TPU v7x, 128 devices: a whole 4x4x4 slice. The times are simulated.
128 devices in a mesh: section: 2 (over core), tp: 4 (over x), rep: 16 (over z, y).
Axes of the slice: x: 4, y: 4, z: 4, core: 2. Of those that a mesh axis runs over, the one named last changes fastest.
Arguments:
- embeddings: bfloat16 [1024, 4096], P(None, 'tp')
- norm_gain: float32 [2, 4096], P('section'), may hold values from 0.25 to 1.75
- query_weight: bfloat16 [2, 4096, 2048], P('section', 'rep', 'tp')
- key_weight: bfloat16 [2, 4096, 1024], P('section', 'rep', 'tp')
- value_weight: bfloat16 [2, 4096, 1024], P('section', 'rep', 'tp'), may hold values from -0.09375 to 0.09375
- out_weight: bfloat16 [2, 2048, 4096], P('section', 'rep', 'tp'), may hold values from -0.25 to 0.25
- group_blocks: int32 [8], replicated, may hold values from 1 to 16, 64 in all
Outputs:
- final_state: bfloat16 [1024, 4096], P('section', 'tp')
Inputs may be any that keep to these rules, and one draw needn't show every extreme that they name: `group_blocks`: the entries sum to 64, and the largest is exactly 16.
All inputs are finite; a program needn't handle non-finite values.
Results may differ from a plain program's by a relative error of at most 0.027.
Values may be sent and summed in bfloat16 or wider, within the bound.
A program may use at most 64 MiB of HBM per device.

v0:
```python
import math

import jax
import jax.numpy as jnp
from jax import lax
from jax.sharding import PartitionSpec as P

HEAD = 128
GROUPS = 8
UNIT = 16
LOOK = 2
SEQ = 1024


def from_behind(block, axis, distance):
    devices = range(lax.axis_size(axis))
    route = [(i - distance, i) for i in devices if i - distance in devices]
    return lax.ppermute(block, axis, route)


def broadcast(value, axis, source):
    kept = jnp.where(lax.axis_index(axis) == source, value, 0).astype(value.dtype)
    return lax.psum(kept, axis)


def on_device(
    embeddings, norm_gain, query_weight, key_weight, value_weight, out_weight, group_blocks
):
    phases = lax.axis_size("section")
    phase_index = lax.axis_index("section")
    replicas = lax.axis_size("rep")
    rep_index = lax.axis_index("rep")
    all_query, all_key, all_value, all_out = (
        lax.all_gather(query_weight, "rep", axis=1, tiled=True),
        lax.all_gather(key_weight, "rep", axis=1, tiled=True),
        lax.all_gather(value_weight, "rep", axis=1, tiled=True),
        lax.all_gather(out_weight, "rep", axis=1, tiled=True),
    )
    w_query = all_query[0]
    w_key = all_key[0]
    w_value = all_value[0]
    w_out = all_out[0]
    gain_row = norm_gain[0]
    feature_width = embeddings.shape[1]
    kv_local = w_key.shape[1] // HEAD
    kv_width = w_key.shape[1]
    query_width = w_query.shape[1]
    longest = SEQ // 4
    buffer_rows = SEQ + longest
    score_scale = 1.0 / math.sqrt(HEAD)
    lengths = group_blocks * UNIT
    starts = jnp.cumsum(lengths) - lengths
    group_slots = jnp.arange(GROUPS, dtype=jnp.int32)
    key_places = jnp.arange(buffer_rows, dtype=jnp.int32)
    key_groups = jnp.sum((key_places[:, None] >= starts[None, 1:]).astype(jnp.int32), axis=1)
    padded = jnp.concatenate(
        [embeddings, jnp.zeros((longest, feature_width), jnp.bfloat16)], axis=0
    )
    block_count = GROUPS
    part_rows = longest // replicas

    def block_start(block_index):
        return jnp.sum(jnp.where(group_slots == block_index, starts, 0))

    def one_tick(tick_index, carry):
        incoming, key_cache, value_cache, collected = carry
        block_index = tick_index - phase_index
        working = (block_index >= 0) & (block_index < block_count)
        row_start = block_start(jnp.clip(block_index, 0, block_count - 1))
        own_start = row_start + rep_index * part_rows
        embedded_block = lax.dynamic_slice_in_dim(padded, own_start, part_rows, 0)
        own_rows = jnp.where(phase_index == 0, embedded_block, incoming)
        full_rows = lax.all_gather(own_rows, "tp", axis=1, tiled=True)

        def project_rows(rows):
            widened = rows.astype(jnp.float32)
            inverse = lax.rsqrt(jnp.mean(widened * widened, axis=1, keepdims=True) + 1e-05)
            normed = (widened * inverse * gain_row).astype(jnp.bfloat16)
            queries = jnp.dot(normed, w_query, preferred_element_type=jnp.float32).astype(
                jnp.bfloat16
            )
            key_rows = jnp.dot(normed, w_key, preferred_element_type=jnp.float32).astype(
                jnp.bfloat16
            )
            value_rows = jnp.dot(normed, w_value, preferred_element_type=jnp.float32).astype(
                jnp.bfloat16
            )
            return (queries, key_rows, value_rows)

        def skip_rows(rows):
            return (
                jnp.zeros((part_rows, query_width), jnp.bfloat16),
                jnp.zeros((part_rows, kv_width), jnp.bfloat16),
                jnp.zeros((part_rows, kv_width), jnp.bfloat16),
            )

        queries, key_rows, value_rows = lax.cond(working, project_rows, skip_rows, full_rows)
        block_keys, block_values = (
            lax.all_gather(key_rows, "rep", axis=0, tiled=True),
            lax.all_gather(value_rows, "rep", axis=0, tiled=True),
        )
        old_keys = lax.dynamic_slice_in_dim(key_cache, row_start, longest, 0)
        old_values = lax.dynamic_slice_in_dim(value_cache, row_start, longest, 0)
        key_cache = lax.dynamic_update_slice_in_dim(
            key_cache, jnp.where(working, block_keys, old_keys), row_start, 0
        )
        value_cache = lax.dynamic_update_slice_in_dim(
            value_cache, jnp.where(working, block_values, old_values), row_start, 0
        )

        def attend_rows(operands):
            query_rows, cache_keys, cache_values = operands
            query_places = own_start + jnp.arange(part_rows, dtype=jnp.int32)
            query_groups = jnp.sum(
                (query_places[:, None] >= starts[None, 1:]).astype(jnp.int32), axis=1
            )
            allowed = (key_places[None, :] <= query_places[:, None]) & (
                key_groups[None, :] >= query_groups[:, None] - LOOK
            )
            query_heads = query_rows.reshape(part_rows, kv_local, 2, HEAD)
            key_heads = cache_keys.reshape(buffer_rows, kv_local, HEAD)
            value_heads = cache_values.reshape(buffer_rows, kv_local, HEAD)
            scores = (
                jnp.einsum(
                    "qgrd,kgd->grqk", query_heads, key_heads, preferred_element_type=jnp.float32
                )
                * score_scale
            )
            scores = jnp.where(allowed[None, None], scores, -jnp.inf)
            weights = jax.nn.softmax(scores, axis=-1).astype(jnp.bfloat16)
            attended = jnp.einsum(
                "grqk,kgd->qgrd", weights, value_heads, preferred_element_type=jnp.float32
            )
            return attended.astype(jnp.bfloat16).reshape(part_rows, kv_local * 2 * HEAD)

        def skip_attend(operands):
            return jnp.zeros((part_rows, kv_local * 2 * HEAD), jnp.bfloat16)

        attended = lax.cond(working, attend_rows, skip_attend, (queries, key_cache, value_cache))
        starting = jnp.zeros((part_rows, feature_width), jnp.float32)
        received = lax.all_gather(attended, "tp", axis=1, tiled=True)

        def product(total):
            return jnp.dot(received, w_out, preferred_element_type=jnp.float32)

        def unchanged(total):
            return total

        projected = lax.cond(working, product, unchanged, starting)
        summed = (own_rows.astype(jnp.float32) + projected).astype(jnp.bfloat16)
        updated = jnp.where(working, summed, jnp.zeros_like(summed))
        old_rows = lax.dynamic_slice_in_dim(collected, own_start, part_rows, 0)
        collected = lax.dynamic_update_slice_in_dim(
            collected, jnp.where(working, updated, old_rows), own_start, 0
        )
        incoming = from_behind(updated, "section", 1)
        return (incoming, key_cache, value_cache, collected)

    start_carry = (
        jnp.zeros((part_rows, feature_width), jnp.bfloat16),
        jnp.zeros((buffer_rows, kv_width), jnp.bfloat16),
        jnp.zeros((buffer_rows, kv_width), jnp.bfloat16),
        jnp.zeros((buffer_rows, feature_width), jnp.bfloat16),
    )
    final_carry = lax.fori_loop(0, block_count + phases - 1, one_tick, start_carry)
    collected = final_carry[3]
    shown = broadcast(collected[:SEQ], "section", phases - 1)
    per_phase = SEQ // phases
    mine = lax.dynamic_slice_in_dim(shown, phase_index * per_phase, per_phase, 0)
    both_halves = lax.all_gather(mine, "rep", axis=1, tiled=True)
    out_places = phase_index * per_phase + jnp.arange(per_phase, dtype=jnp.int32)
    out_groups = jnp.sum((out_places[:, None] >= starts[None, 1:]).astype(jnp.int32), axis=1)
    out_starts = jnp.sum(
        jnp.where(out_groups[:, None] == group_slots[None, :], starts[None, :], 0), axis=1
    )
    owners = (out_places - out_starts) // part_rows
    pieces = both_halves.reshape(per_phase, replicas, feature_width)
    owner_match = owners[:, None, None] == jnp.arange(replicas, dtype=jnp.int32)[None, :, None]
    chosen = jnp.where(owner_match, pieces, jnp.zeros_like(pieces))
    return jnp.sum(chosen.astype(jnp.float32), axis=1).astype(jnp.bfloat16)


def solution(mesh):
    in_specs = (
        P(None, "tp"),
        P("section", None),
        P("section", "rep", "tp"),
        P("section", "rep", "tp"),
        P("section", "rep", "tp"),
        P("section", "rep", "tp"),
        P(),
    )
    out_specs = P("section", "tp")
    return jax.shard_map(
        on_device, mesh=mesh, in_specs=in_specs, out_specs=out_specs, check_vma=False
    )
```

profile of v0, /device:TPU:1, one launch (start us, length us, event | category | flops | bytes accessed | tf_op | source)
XLA Modules:
  0.0 1253.7 jit_solution(14419658658636608760)
XLA Ops:
  16.2 40.8 %all-gather.8.cloned.1.call-done = bf16[1,4096,256]{2,1,0:T(8,128)(2,1)} async-done(((bf16[1,256,256]{2,1,0:T(8,128)(2,1)}), bf16[1,4096,256]{2,1,0:T(8,128)(2,1)}) %all-gather.8.cloned.1.call-update) | async-done | bytes 2097168 | tf_op jit(solution)/shard_map/all_gather | solution.py:35
  57.0 46.7 %all-gather.10.cloned.1.call-done = bf16[1,4096,256]{2,1,0:T(8,128)(2,1)} async-done(((bf16[1,256,256]{2,1,0:T(8,128)(2,1)}), bf16[1,4096,256]{2,1,0:T(8,128)(2,1)}) %all-gather.10.cloned.1.call-update) | async-done | bytes 2097168 | tf_op jit(solution)/shard_map/all_gather | solution.py:36
  103.7 54.1 %all-gather.12.cloned.1.call-done = bf16[1,2048,1024]{2,1,0:T(8,128)(2,1)} async-done(((bf16[1,128,1024]{2,1,0:T(8,128)(2,1)}), bf16[1,2048,1024]{2,1,0:T(8,128)(2,1)}) %all-gather.12.cloned.1.call-update) | async-done | bytes 4194320 | tf_op jit(solution)/shard_map/all_gather | solution.py:37
  157.8 53.3 %all-gather.6.cloned.1.call-done = bf16[1,4096,512]{2,1,0:T(8,128)(2,1)} async-done(((bf16[1,256,512]{2,1,0:T(8,128)(2,1)}), bf16[1,4096,512]{2,1,0:T(8,128)(2,1)}) %all-gather.6.cloned.1.call-update) | async-done | bytes 4194320 | tf_op jit(solution)/shard_map/all_gather | solution.py:34
  213.1 866.0 %while.22 = (s32[]{:T(128)}, bf16[16,1024]{1,0:T(8,128)(2,1)S(1)}, bf16[1280,256]{1,0:T(8,128)(2,1)S(1)}, bf16[1280,256]{1,0:T(8,128)(2,1)S(1)}, bf16[1280,1024]...) while((s32[]{:T(128)}, bf16[16,1024]{1,0:T(8,128)(2,1)S(1)}, ...), condition=%wide.region_16.17_spmd.clone, body=%wide.region_4.16_spmd.clone.sunk | while | flops 245144528 | bytes 30811276 | solution.py:165
  217.8 9.4 all_gather.64
  228.4 17.8 %all_gather.66 = bf16[256,256]{1,0:T(8,128)(2,1)S(1)} all-gather(bf16[16,256]{1,0:T(8,128)(2,1)S(1)} %get-tuple-element.631), channel_id=1, replica_groups=mesh['section'=2,'tp'=4,'rep'=16] {'rep'}, dimensions={0}, use_global_device_ids=true | all-gather | bytes 139264 | tf_op jit(solution)/shard_map/while/body/eval_jaxpr/all_gather | solution.py:100
  249.4 16.1 %all_gather.65 = bf16[256,256]{1,0:T(8,128)(2,1)S(1)} all-gather(bf16[16,256]{1,0:T(8,128)(2,1)} %copy-done.7), channel_id=1, replica_groups=mesh['section'=2,'tp'=4,'rep'=16] {'rep'}, dimensions={0}, use_global_device_ids=true | all-gather | bytes 139264 | tf_op jit(solution)/shard_map/while/body/eval_jaxpr/all_gather | solution.py:99
  280.0 31.7 %collective-permute-done = bf16[16,1024]{1,0:T(8,128)(2,1)S(1)} collective-permute-done((bf16[16,1024]{1,0:T(8,128)(2,1)S(1)}, bf16[16,1024]{1,0:T(8,128)(2,1)S(1)}, u32[]{:S(2)}, u32[]{:S(2)}) %collective-permute-start) | collective-permute-done | bytes 32800 | tf_op jit(solution)/shard_map/while/body/eval_jaxpr/ppermute | solution.py:18
  316.3 9.2 all_gather.64
  330.7 17.5 %all_gather.66 = bf16[256,256]{1,0:T(8,128)(2,1)S(1)} all-gather(bf16[16,256]{1,0:T(8,128)(2,1)S(1)} %get-tuple-element.631), channel_id=1, replica_groups=mesh['section'=2,'tp'=4,'rep'=16] {'rep'}, dimensions={0}, use_global_device_ids=true | all-gather | bytes 139264 | tf_op jit(solution)/shard_map/while/body/eval_jaxpr/all_gather | solution.py:100
  351.3 16.4 %all_gather.65 = bf16[256,256]{1,0:T(8,128)(2,1)S(1)} all-gather(bf16[16,256]{1,0:T(8,128)(2,1)} %copy-done.7), channel_id=1, replica_groups=mesh['section'=2,'tp'=4,'rep'=16] {'rep'}, dimensions={0}, use_global_device_ids=true | all-gather | bytes 139264 | tf_op jit(solution)/shard_map/while/body/eval_jaxpr/all_gather | solution.py:99
  377.3 9.0 all_gather.67
  393.4 16.2 %collective-permute-done = bf16[16,1024]{1,0:T(8,128)(2,1)S(1)} collective-permute-done((bf16[16,1024]{1,0:T(8,128)(2,1)S(1)}, bf16[16,1024]{1,0:T(8,128)(2,1)S(1)}, u32[]{:S(2)}, u32[]{:S(2)}) %collective-permute-start) | collective-permute-done | bytes 32800 | tf_op jit(solution)/shard_map/while/body/eval_jaxpr/ppermute | solution.py:18
  414.2 9.2 all_gather.64
  428.6 17.5 %all_gather.66 = bf16[256,256]{1,0:T(8,128)(2,1)S(1)} all-gather(bf16[16,256]{1,0:T(8,128)(2,1)S(1)} %get-tuple-element.631), channel_id=1, replica_groups=mesh['section'=2,'tp'=4,'rep'=16] {'rep'}, dimensions={0}, use_global_device_ids=true | all-gather | bytes 139264 | tf_op jit(solution)/shard_map/while/body/eval_jaxpr/all_gather | solution.py:100
  449.2 16.4 %all_gather.65 = bf16[256,256]{1,0:T(8,128)(2,1)S(1)} all-gather(bf16[16,256]{1,0:T(8,128)(2,1)} %copy-done.7), channel_id=1, replica_groups=mesh['section'=2,'tp'=4,'rep'=16] {'rep'}, dimensions={0}, use_global_device_ids=true | all-gather | bytes 139264 | tf_op jit(solution)/shard_map/while/body/eval_jaxpr/all_gather | solution.py:99
  475.1 9.0 all_gather.67
  491.2 16.3 %collective-permute-done = bf16[16,1024]{1,0:T(8,128)(2,1)S(1)} collective-permute-done((bf16[16,1024]{1,0:T(8,128)(2,1)S(1)}, bf16[16,1024]{1,0:T(8,128)(2,1)S(1)}, u32[]{:S(2)}, u32[]{:S(2)}) %collective-permute-start) | collective-permute-done | bytes 32800 | tf_op jit(solution)/shard_map/while/body/eval_jaxpr/ppermute | solution.py:18
  512.2 9.1 all_gather.64
  526.5 17.5 %all_gather.66 = bf16[256,256]{1,0:T(8,128)(2,1)S(1)} all-gather(bf16[16,256]{1,0:T(8,128)(2,1)S(1)} %get-tuple-element.631), channel_id=1, replica_groups=mesh['section'=2,'tp'=4,'rep'=16] {'rep'}, dimensions={0}, use_global_device_ids=true | all-gather | bytes 139264 | tf_op jit(solution)/shard_map/while/body/eval_jaxpr/all_gather | solution.py:100
  547.1 16.4 %all_gather.65 = bf16[256,256]{1,0:T(8,128)(2,1)S(1)} all-gather(bf16[16,256]{1,0:T(8,128)(2,1)} %copy-done.7), channel_id=1, replica_groups=mesh['section'=2,'tp'=4,'rep'=16] {'rep'}, dimensions={0}, use_global_device_ids=true | all-gather | bytes 139264 | tf_op jit(solution)/shard_map/while/body/eval_jaxpr/all_gather | solution.py:99
  573.1 9.0 all_gather.67
  589.2 16.3 %collective-permute-done = bf16[16,1024]{1,0:T(8,128)(2,1)S(1)} collective-permute-done((bf16[16,1024]{1,0:T(8,128)(2,1)S(1)}, bf16[16,1024]{1,0:T(8,128)(2,1)S(1)}, u32[]{:S(2)}, u32[]{:S(2)}) %collective-permute-start) | collective-permute-done | bytes 32800 | tf_op jit(solution)/shard_map/while/body/eval_jaxpr/ppermute | solution.py:18
  610.1 9.2 all_gather.64
  624.5 17.5 %all_gather.66 = bf16[256,256]{1,0:T(8,128)(2,1)S(1)} all-gather(bf16[16,256]{1,0:T(8,128)(2,1)S(1)} %get-tuple-element.631), channel_id=1, replica_groups=mesh['section'=2,'tp'=4,'rep'=16] {'rep'}, dimensions={0}, use_global_device_ids=true | all-gather | bytes 139264 | tf_op jit(solution)/shard_map/while/body/eval_jaxpr/all_gather | solution.py:100
  645.0 16.4 %all_gather.65 = bf16[256,256]{1,0:T(8,128)(2,1)S(1)} all-gather(bf16[16,256]{1,0:T(8,128)(2,1)} %copy-done.7), channel_id=1, replica_groups=mesh['section'=2,'tp'=4,'rep'=16] {'rep'}, dimensions={0}, use_global_device_ids=true | all-gather | bytes 139264 | tf_op jit(solution)/shard_map/while/body/eval_jaxpr/all_gather | solution.py:99
  671.0 9.0 all_gather.67
  687.1 16.3 %collective-permute-done = bf16[16,1024]{1,0:T(8,128)(2,1)S(1)} collective-permute-done((bf16[16,1024]{1,0:T(8,128)(2,1)S(1)}, bf16[16,1024]{1,0:T(8,128)(2,1)S(1)}, u32[]{:S(2)}, u32[]{:S(2)}) %collective-permute-start) | collective-permute-done | bytes 32800 | tf_op jit(solution)/shard_map/while/body/eval_jaxpr/ppermute | solution.py:18
  708.0 9.2 all_gather.64
  722.4 17.5 %all_gather.66 = bf16[256,256]{1,0:T(8,128)(2,1)S(1)} all-gather(bf16[16,256]{1,0:T(8,128)(2,1)S(1)} %get-tuple-element.631), channel_id=1, replica_groups=mesh['section'=2,'tp'=4,'rep'=16] {'rep'}, dimensions={0}, use_global_device_ids=true | all-gather | bytes 139264 | tf_op jit(solution)/shard_map/while/body/eval_jaxpr/all_gather | solution.py:100
  743.0 16.4 %all_gather.65 = bf16[256,256]{1,0:T(8,128)(2,1)S(1)} all-gather(bf16[16,256]{1,0:T(8,128)(2,1)} %copy-done.7), channel_id=1, replica_groups=mesh['section'=2,'tp'=4,'rep'=16] {'rep'}, dimensions={0}, use_global_device_ids=true | all-gather | bytes 139264 | tf_op jit(solution)/shard_map/while/body/eval_jaxpr/all_gather | solution.py:99
  768.9 9.0 all_gather.67
  785.0 16.3 %collective-permute-done = bf16[16,1024]{1,0:T(8,128)(2,1)S(1)} collective-permute-done((bf16[16,1024]{1,0:T(8,128)(2,1)S(1)}, bf16[16,1024]{1,0:T(8,128)(2,1)S(1)}, u32[]{:S(2)}, u32[]{:S(2)}) %collective-permute-start) | collective-permute-done | bytes 32800 | tf_op jit(solution)/shard_map/while/body/eval_jaxpr/ppermute | solution.py:18
  805.9 9.2 all_gather.64
  820.3 17.4 %all_gather.66 = bf16[256,256]{1,0:T(8,128)(2,1)S(1)} all-gather(bf16[16,256]{1,0:T(8,128)(2,1)S(1)} %get-tuple-element.631), channel_id=1, replica_groups=mesh['section'=2,'tp'=4,'rep'=16] {'rep'}, dimensions={0}, use_global_device_ids=true | all-gather | bytes 139264 | tf_op jit(solution)/shard_map/while/body/eval_jaxpr/all_gather | solution.py:100
  840.9 16.3 %all_gather.65 = bf16[256,256]{1,0:T(8,128)(2,1)S(1)} all-gather(bf16[16,256]{1,0:T(8,128)(2,1)} %copy-done.7), channel_id=1, replica_groups=mesh['section'=2,'tp'=4,'rep'=16] {'rep'}, dimensions={0}, use_global_device_ids=true | all-gather | bytes 139264 | tf_op jit(solution)/shard_map/while/body/eval_jaxpr/all_gather | solution.py:99
  882.9 16.3 %collective-permute-done = bf16[16,1024]{1,0:T(8,128)(2,1)S(1)} collective-permute-done((bf16[16,1024]{1,0:T(8,128)(2,1)S(1)}, bf16[16,1024]{1,0:T(8,128)(2,1)S(1)}, u32[]{:S(2)}, u32[]{:S(2)}) %collective-permute-start) | collective-permute-done | bytes 32800 | tf_op jit(solution)/shard_map/while/body/eval_jaxpr/ppermute | solution.py:18
  903.9 9.1 all_gather.64
  918.2 17.5 %all_gather.66 = bf16[256,256]{1,0:T(8,128)(2,1)S(1)} all-gather(bf16[16,256]{1,0:T(8,128)(2,1)S(1)} %get-tuple-element.631), channel_id=1, replica_groups=mesh['section'=2,'tp'=4,'rep'=16] {'rep'}, dimensions={0}, use_global_device_ids=true | all-gather | bytes 139264 | tf_op jit(solution)/shard_map/while/body/eval_jaxpr/all_gather | solution.py:100
  938.8 16.3 %all_gather.65 = bf16[256,256]{1,0:T(8,128)(2,1)S(1)} all-gather(bf16[16,256]{1,0:T(8,128)(2,1)} %copy-done.7), channel_id=1, replica_groups=mesh['section'=2,'tp'=4,'rep'=16] {'rep'}, dimensions={0}, use_global_device_ids=true | all-gather | bytes 139264 | tf_op jit(solution)/shard_map/while/body/eval_jaxpr/all_gather | solution.py:99
  980.8 16.0 %collective-permute-done = bf16[16,1024]{1,0:T(8,128)(2,1)S(1)} collective-permute-done((bf16[16,1024]{1,0:T(8,128)(2,1)S(1)}, bf16[16,1024]{1,0:T(8,128)(2,1)S(1)}, u32[]{:S(2)}, u32[]{:S(2)}) %collective-permute-start) | collective-permute-done | bytes 32800 | tf_op jit(solution)/shard_map/while/body/eval_jaxpr/ppermute | solution.py:18
  1001.4 9.1 all_gather.64
  1015.7 17.4 %all_gather.66 = bf16[256,256]{1,0:T(8,128)(2,1)S(1)} all-gather(bf16[16,256]{1,0:T(8,128)(2,1)S(1)} %get-tuple-element.631), channel_id=1, replica_groups=mesh['section'=2,'tp'=4,'rep'=16] {'rep'}, dimensions={0}, use_global_device_ids=true | all-gather | bytes 139264 | tf_op jit(solution)/shard_map/while/body/eval_jaxpr/all_gather | solution.py:100
  1036.2 16.4 %all_gather.65 = bf16[256,256]{1,0:T(8,128)(2,1)S(1)} all-gather(bf16[16,256]{1,0:T(8,128)(2,1)} %copy-done.7), channel_id=1, replica_groups=mesh['section'=2,'tp'=4,'rep'=16] {'rep'}, dimensions={0}, use_global_device_ids=true | all-gather | bytes 139264 | tf_op jit(solution)/shard_map/while/body/eval_jaxpr/all_gather | solution.py:99
  1082.3 25.8 %all-reduce.3.cloned.1.call-done = bf16[1024,1024]{1,0:T(8,128)(2,1)} async-done(((bf16[1024,1024]{1,0:T(8,128)(2,1)}), bf16[1024,1024]{1,0:T(8,128)(2,1)}) %all-reduce.3.cloned.1.call-update) | async-done | bytes 2097168 | tf_op jit(solution)/shard_map/psum | solution.py:23
  1111.3 111.5 %all-gather.14.cloned.1.call-done = bf16[512,16384]{1,0:T(8,128)(2,1)} async-done(((bf16[512,1024]{1,0:T(8,128)(2,1)}), bf16[512,16384]{1,0:T(8,128)(2,1)}) %all-gather.14.cloned.1.call-update) | async-done | bytes 16777232 | tf_op jit(solution)/shard_map/all_gather | solution.py:170
  1222.8 15.6 %copy.25 = bf16[64,8,16,1024]{3,2,1,0:T(8,128)(2,1)S(1)} copy(bf16[64,8,16,1024]{3,1,2,0:T(8,128)(2,1)} %bitcast.33) | data formatting | bytes 33554432
  (421 shorter events, 417.7 us)
Async XLA Ops:
  6.5 50.5 %all-gather.8.cloned.1.call-start = ((), (), s32[]{:S(2)}) async-start(), calls=%async_computation.1 | async-start | bytes 2228224 | tf_op jit(solution)/shard_map/all_gather | solution.py:35
  7.3 96.4 %all-gather.10.cloned.1.call-start = ((), (), s32[]{:S(2)}) async-start(), calls=%async_computation.2 | async-start | bytes 2228224 | tf_op jit(solution)/shard_map/all_gather | solution.py:36
  8.0 149.8 %all-gather.12.cloned.1.call-start = ((), (), s32[]{:S(2)}) async-start(), calls=%async_computation.3 | async-start | bytes 4456448 | tf_op jit(solution)/shard_map/all_gather | solution.py:37
  8.7 202.4 %all-gather.6.cloned.1.call-start = ((), (), s32[]{:S(2)}) async-start(), calls=%async_computation | async-start | bytes 4456448 | tf_op jit(solution)/shard_map/all_gather | solution.py:34
  9.3 1098.7 %all-reduce.3.cloned.1.call-start = ((), (), s32[]{:S(2)}) async-start(), calls=%async_computation.4 | async-start | bytes 4194304 | tf_op jit(solution)/shard_map/psum | solution.py:23
  12.1 4.1 copy-start.8
  15.5 197.6 %copy-start.5 = (f32[1,4096]{1,0:T(1,128)S(1)}, f32[1,4096]{1,0:T(1,128)}, u32[]{:S(2)}) copy-start(f32[1,4096]{1,0:T(1,128)} %param.16) | copy-start | bytes 49156
  57.0 156.1 %copy-start = (bf16[1,4096,256]{2,1,0:T(8,128)(2,1)S(1)}, bf16[1,4096,256]{2,1,0:T(8,128)(2,1)}, u32[]{:S(2)}) copy-start(bf16[1,4096,256]{2,1,0:T(8,128)(2,1)} %all-gather.8.cloned.1.call-done) | copy-start | bytes 6291460
  266.7 9.6 copy-start.4
  277.2 34.4 %collective-permute-start = (bf16[16,1024]{1,0:T(8,128)(2,1)S(1)}, bf16[16,1024]{1,0:T(8,128)(2,1)S(1)}, u32[]{:S(2)}, u32[]{:S(2)}) collective-permute-start(bf16[16,1024]{1,0:T(8,128)(2,1)S(1)} %get-tuple-element.632), channel_id=1, source_target_pairs={{0,64},{1,65},{2,66},{3,67},{4,68},{5,69},{6,70},{7,71},{8,72},{9,... | collective-permute-start | bytes 98312 | tf_op jit(solution)/shard_map/while/body/eval_jaxpr/ppermute | solution.py:18
  325.5 3.2 copy-start.1
  329.5 0.6 copy-start.6
  373.7 0.7 copy-start.2
  377.3 12.5 copy-start.4
  390.6 19.0 %collective-permute-start = (bf16[16,1024]{1,0:T(8,128)(2,1)S(1)}, bf16[16,1024]{1,0:T(8,128)(2,1)S(1)}, u32[]{:S(2)}, u32[]{:S(2)}) collective-permute-start(bf16[16,1024]{1,0:T(8,128)(2,1)S(1)} %get-tuple-element.632), channel_id=1, source_target_pairs={{0,64},{1,65},{2,66},{3,67},{4,68},{5,69},{6,70},{7,71},{8,72},{9,... | collective-permute-start | bytes 98312 | tf_op jit(solution)/shard_map/while/body/eval_jaxpr/ppermute | solution.py:18
  423.4 3.2 copy-start.1
  471.5 0.7 copy-start.2
  475.1 12.5 copy-start.4
  488.5 19.0 %collective-permute-start = (bf16[16,1024]{1,0:T(8,128)(2,1)S(1)}, bf16[16,1024]{1,0:T(8,128)(2,1)S(1)}, u32[]{:S(2)}, u32[]{:S(2)}) collective-permute-start(bf16[16,1024]{1,0:T(8,128)(2,1)S(1)} %get-tuple-element.632), channel_id=1, source_target_pairs={{0,64},{1,65},{2,66},{3,67},{4,68},{5,69},{6,70},{7,71},{8,72},{9,... | collective-permute-start | bytes 98312 | tf_op jit(solution)/shard_map/while/body/eval_jaxpr/ppermute | solution.py:18
  521.3 3.2 copy-start.1
  525.3 0.6 copy-start.6
  569.5 0.7 copy-start.2
  573.0 12.5 copy-start.4
  586.4 19.0 %collective-permute-start = (bf16[16,1024]{1,0:T(8,128)(2,1)S(1)}, bf16[16,1024]{1,0:T(8,128)(2,1)S(1)}, u32[]{:S(2)}, u32[]{:S(2)}) collective-permute-start(bf16[16,1024]{1,0:T(8,128)(2,1)S(1)} %get-tuple-element.632), channel_id=1, source_target_pairs={{0,64},{1,65},{2,66},{3,67},{4,68},{5,69},{6,70},{7,71},{8,72},{9,... | collective-permute-start | bytes 98312 | tf_op jit(solution)/shard_map/while/body/eval_jaxpr/ppermute | solution.py:18
  619.2 3.2 copy-start.1
  623.3 0.6 copy-start.6
  667.4 0.7 copy-start.2
  671.0 12.5 copy-start.4
  684.3 19.0 %collective-permute-start = (bf16[16,1024]{1,0:T(8,128)(2,1)S(1)}, bf16[16,1024]{1,0:T(8,128)(2,1)S(1)}, u32[]{:S(2)}, u32[]{:S(2)}) collective-permute-start(bf16[16,1024]{1,0:T(8,128)(2,1)S(1)} %get-tuple-element.632), channel_id=1, source_target_pairs={{0,64},{1,65},{2,66},{3,67},{4,68},{5,69},{6,70},{7,71},{8,72},{9,... | collective-permute-start | bytes 98312 | tf_op jit(solution)/shard_map/while/body/eval_jaxpr/ppermute | solution.py:18
  717.2 3.2 copy-start.1
  721.2 0.6 copy-start.6
  765.3 0.7 copy-start.2
  768.9 12.5 copy-start.4
  782.3 19.0 %collective-permute-start = (bf16[16,1024]{1,0:T(8,128)(2,1)S(1)}, bf16[16,1024]{1,0:T(8,128)(2,1)S(1)}, u32[]{:S(2)}, u32[]{:S(2)}) collective-permute-start(bf16[16,1024]{1,0:T(8,128)(2,1)S(1)} %get-tuple-element.632), channel_id=1, source_target_pairs={{0,64},{1,65},{2,66},{3,67},{4,68},{5,69},{6,70},{7,71},{8,72},{9,... | collective-permute-start | bytes 98312 | tf_op jit(solution)/shard_map/while/body/eval_jaxpr/ppermute | solution.py:18
  815.1 3.2 copy-start.1
  863.2 0.7 copy-start.2
  866.8 12.5 copy-start.4
  880.2 19.1 %collective-permute-start = (bf16[16,1024]{1,0:T(8,128)(2,1)S(1)}, bf16[16,1024]{1,0:T(8,128)(2,1)S(1)}, u32[]{:S(2)}, u32[]{:S(2)}) collective-permute-start(bf16[16,1024]{1,0:T(8,128)(2,1)S(1)} %get-tuple-element.632), channel_id=1, source_target_pairs={{0,64},{1,65},{2,66},{3,67},{4,68},{5,69},{6,70},{7,71},{8,72},{9,... | collective-permute-start | bytes 98312 | tf_op jit(solution)/shard_map/while/body/eval_jaxpr/ppermute | solution.py:18
  913.0 3.2 copy-start.1
  961.1 0.7 copy-start.2
  964.6 12.5 copy-start.4
  978.0 18.7 %collective-permute-start = (bf16[16,1024]{1,0:T(8,128)(2,1)S(1)}, bf16[16,1024]{1,0:T(8,128)(2,1)S(1)}, u32[]{:S(2)}, u32[]{:S(2)}) collective-permute-start(bf16[16,1024]{1,0:T(8,128)(2,1)S(1)} %get-tuple-element.632), channel_id=1, source_target_pairs={{0,64},{1,65},{2,66},{3,67},{4,68},{5,69},{6,70},{7,71},{8,72},{9,... | collective-permute-start | bytes 98312 | tf_op jit(solution)/shard_map/while/body/eval_jaxpr/ppermute | solution.py:18
  1010.5 3.2 copy-start.1
  1058.3 0.7 copy-start.2
  1061.9 12.5 copy-start.4
  1075.2 3.9 collective-permute-start
  1082.2 28.2 %copy-start.9 = (s32[7]{0:T(128)S(1)}, s32[7]{0:T(128)}, u32[]{:S(2)}) copy-start(s32[7]{0:T(128)} %copy-done.8) | copy-start | bytes 88
  1082.2 140.6 %all-gather.14.cloned.1.call-start = ((), (), s32[]{:S(2)}) async-start(), calls=%async_computation.5 | async-start | bytes 17825792 | tf_op jit(solution)/shard_map/all_gather | solution.py:170
  (23 other events, 13.8 us)
Sparse Core Ops, SparseCore 0:
  9.5 47.4 all-gather.7
  59.1 44.5 all-gather.9
  105.8 51.9 all-gather.11
  159.8 51.2 all-gather.5
  1082.3 25.6 all-reduce.2
  1110.5 112.3 all-gather.13
where the time goes:
time: 1260 us; the launch traced here: 1250 us
  waiting for transfers between devices  481 us (38%)
  blocking collectives  468 us (37%)
  local copies, waits for them, and re-layouts  113 us (9%)
  matrix products  82.8 us (7%)
  other arithmetic  58.8 us (5%)
  loops' own time  24.7 us (2%)
  between operations  13.6 us (1%)
    all_gather x9, blocking collectives, one_tick(): lax.all_gather(value_rows, 'rep', axis=0, tiled=True)  158 us
    all_gather x9, blocking collectives, one_tick(): lax.all_gather(key_rows, 'rep', axis=0, tiled=True)  147 us
    ppermute x9, waiting for transfers between devices, from_behind(): return lax.ppermute(block, axis, route)  146 us
    all_gather x1, waiting for transfers between devices, on_device(): both_halves = lax.all_gather(mine, 'rep', axis=1, tiled=True)  112 us
    all_gather x9, blocking collectives, one_tick(): full_rows = lax.all_gather(own_rows, 'tp', axis=1, tiled=True)  82.6 us
    all_gather x9, blocking collectives, one_tick(): received = lax.all_gather(attended, 'tp', axis=1, tiled=True)  80.8 us
    all_gather x1, waiting for transfers between devices, on_device(): lax.all_gather(out_weight, 'rep', axis=1, tiled=True)  54.1 us
    all_gather x1, waiting for transfers between devices, on_device(): lax.all_gather(query_weight, 'rep', axis=1, tiled=True)  53.3 us
  transfers between devices with their start and end apart: 15, of which 15 were waited for; matrix products, arithmetic and copies ran while one was open for 2% of the time, Pallas kernels for 0%

commit v1 on v0

v1 whole, which is shorter than its diff:
```python
import math

import jax
import jax.numpy as jnp
from jax import lax
from jax.experimental import pallas as pl
from jax.experimental.pallas import tpu as pltpu
from jax.sharding import PartitionSpec as P

MESH = pl.DeviceIdType.MESH
BF = jnp.bfloat16
F32 = jnp.float32
D = 4096
GROUPS = 8
UNIT = 16
SCALE = 1.0 / math.sqrt(128)

W_LEFT, W_RIGHT, W_FAR = 0, 3, 6
O_LEFT, O_RIGHT, O_FAR = 9, 10, 11
X_IN = 13
RS_IN, SQ_IN = 17, 20
KV_IN = 23
AT_IN = 30
RO_IN = 34
RES_IN = 37
FA_IN, FAY_IN = 38, 42
FB_IN, FBZ_IN = 45, 49
N_RECV = 55
N_SEND = 72
N_LOCAL = 8


def kernel(
    emb, gain, wq, wk, wv, wo, blocks, out,
    WQ, WK, WV, WO, X, XG, ACC, PS, PR, SQ, SQR, KV, AT, ATR, OS, OR, RES, ST, FIN,
    send_sems, recv_sems, local_sems, go,
):
    s = lax.axis_index("section")
    t = lax.axis_index("tp")
    r = lax.axis_index("rep")
    z = r // 4
    y = r % 4
    g = z // 2
    zh = z % 2
    first = s == 0
    second = s == 1

    def dev(s_, t_, z_, y_):
        return (s_, t_, z_ * 4 + y_)

    def up(v, d):
        return (v + d) % 4

    pending = []

    def send(src, dst, ridx, device, when=None):
        c = pltpu.make_async_remote_copy(
            src_ref=src, dst_ref=dst, send_sem=send_sems.at[len(pending)],
            recv_sem=recv_sems.at[ridx], device_id=device, device_id_type=MESH,
        )
        if when is None:
            c.start()
        else:
            pl.when(when)(c.start)
        pending.append((c, when))

    def arrived(ref, ridx, when=None):
        c = pltpu.make_async_remote_copy(
            src_ref=ref, dst_ref=ref, send_sem=send_sems.at[0],
            recv_sem=recv_sems.at[ridx], device_id=dev(1 - s, t, z, y), device_id_type=MESH,
        )
        if when is None:
            c.wait_recv()
        else:
            pl.when(when)(c.wait_recv)

    def rows(start, size):
        return pl.ds(pl.multiple_of(start, size), size)

    KV[...] = jnp.zeros_like(KV)

    own = [
        pltpu.make_async_copy(wq.at[0], WQ.at[rows(256 * y, 256)], local_sems.at[0]),
        pltpu.make_async_copy(wk.at[0], WK.at[rows(256 * y, 256)], local_sems.at[1]),
        pltpu.make_async_copy(wv.at[0], WV.at[rows(256 * y, 256)], local_sems.at[2]),
        pltpu.make_async_copy(wo.at[0], WO.at[rows(128 * y, 128)], local_sems.at[3]),
    ]
    for c in own:
        c.start()
    x_source = first & (t == z)
    own_x = pltpu.make_async_copy(emb.at[rows(256 * y, 256)], X, local_sems.at[4])
    own_res = pltpu.make_async_copy(emb.at[rows(256 * y + 64 * z, 64)], RES, local_sems.at[5])
    pl.when(x_source)(own_x.start)
    pl.when(first)(own_res.start)

    barrier = pltpu.get_barrier_semaphore()

    def greet(device):
        pl.semaphore_signal(barrier, inc=1, device_id=device, device_id_type=MESH)

    diagonal = z == t
    for d in (1, 2, 3):
        greet(dev(s, t, z, up(y, d)))
        greet(dev(s, t, up(z, d), y))
        greet(dev(s, t, z + 1 - 2 * zh, up(y, d)))
        greet(dev(1 - s, t, z, up(y, d)))
        greet(dev(1 - s, t, up(z, d), y))
        greet(dev(s, up(t, d), t, y))
        greet(dev(s, z, up(z, d), y))
    greet(dev(1 - s, t, z, y))
    greet(dev(s, up(t, 1), z, y))
    greet(dev(s, up(t, 3), z, y))

    @pl.when(jnp.logical_not(diagonal))
    def _():
        greet(dev(s, t, t, y))
        greet(dev(s, z, z, y))

    for d in range(4):
        @pl.when(first)
        def _():
            greet(dev(1, d, t, y))

        @pl.when(second)
        def _():
            greet(dev(0, z, d, y))
    pl.semaphore_wait(barrier, 21 + 1 + 2 + 4 + 2 * (1 - diagonal.astype(jnp.int32)))

    right, left = up(y, 1), up(y, 3)
    dev_r, dev_l = dev(s, t, z, right), dev(s, t, z, left)
    far = up(y, 2)

    half = (X.at[0:128], X.at[128:256])
    dx = (t - z + 4) % 4
    x_right, x_left = dev(s, up(t, 1), z, y), dev(s, up(t, 3), z, y)
    source = [emb.at[rows(256 * y, 128)], emb.at[rows(256 * y + 128, 128)]]
    for i in range(2):
        send(source[i], half[i], X_IN + i, x_right, x_source)
        send(source[1 - i], half[1 - i], X_IN + 1 - i, x_left, x_source)

    @pl.when(second)
    def _():
        pl.semaphore_wait(go, 1)

    at_y = rows(256 * y, 256)
    send(wq.at[0], WQ.at[at_y], W_LEFT, dev_r)
    send(wk.at[0], WK.at[at_y], W_RIGHT + 1, dev_l)
    send(wv.at[0], WV.at[at_y], W_RIGHT + 2, dev_l)
    send(wk.at[0], WK.at[at_y], W_LEFT + 1, dev_r)
    send(wv.at[0], WV.at[at_y], W_LEFT + 2, dev_r)
    send(wq.at[0], WQ.at[at_y], W_RIGHT, dev_l)

    near_right, near_left, opposite = first & (dx == 1), first & (dx == 3), first & (dx == 2)
    arrived(half[0], X_IN, near_right)
    send(half[0], half[0], X_IN, x_right, near_right)
    arrived(half[1], X_IN + 1, near_left)
    send(half[1], half[1], X_IN + 1, x_left, near_left)

    at_l, at_r, at_f = rows(256 * left, 256), rows(256 * right, 256), rows(256 * far, 256)
    arrived(WQ.at[at_l], W_LEFT)
    send(WQ.at[at_l], WQ.at[at_l], W_FAR, dev_r)
    arrived(WK.at[at_r], W_RIGHT + 1)
    send(WK.at[at_r], WK.at[at_r], W_FAR + 1, dev_l)
    arrived(WV.at[at_r], W_RIGHT + 2)
    send(WV.at[at_r], WV.at[at_r], W_FAR + 2, dev_l)

    ow_y = rows(128 * y, 128)
    send(wo.at[0], WO.at[ow_y], O_LEFT, dev_r)
    send(wo.at[0], WO.at[ow_y], O_RIGHT, dev_l)

    pl.when(x_source)(own_x.wait)
    arrived(half[1], X_IN + 1, near_right)
    arrived(half[0], X_IN, near_left)
    arrived(half[0], X_IN, opposite)
    arrived(half[1], X_IN + 1, opposite)
    for c in own:
        c.wait()

    ow_l, ow_r, ow_f = rows(128 * left, 128), rows(128 * right, 128), rows(128 * far, 128)
    lower = lambda start: rows(128 * start, 64)
    upper = lambda start: rows(128 * start + 64, 64)

    def rest_of_out_weights():
        arrived(WO.at[ow_l], O_LEFT)
        arrived(WO.at[ow_r], O_RIGHT)
        send(WO.at[lower(left)], WO.at[lower(left)], O_FAR, dev_r)
        send(WO.at[upper(right)], WO.at[upper(right)], O_FAR + 1, dev_l)

    for zp in range(4):
        arrived(X.at[pl.ds(64 * zp, 64)], X_IN + zp, second)

    x = X[...].astype(F32)
    XG[...] = (x * gain[:, rows(1024 * z, 1024)]).astype(BF)
    squares = jnp.sum(x * x, axis=1, keepdims=True)
    for h in range(2):
        column = jnp.broadcast_to(squares[128 * h:128 * h + 128], (128, 128))
        SQ[h] = jnp.transpose(column)[0:8]

    def multiply(block, start):
        at = rows(256 * block, 256)
        part = XG[:, at]
        for ref, lo, hi in ((WQ, 0, 512), (WK, 512, 768), (WV, 768, 1024)):
            product = jnp.dot(part, ref[at, :], preferred_element_type=F32)
            if start:
                ACC[:, lo:hi] = product
            else:
                ACC[:, lo:hi] += product

    multiply(y, True)
    arrived(WK.at[at_l], W_LEFT + 1)
    arrived(WV.at[at_l], W_LEFT + 2)
    multiply(left, False)
    arrived(WQ.at[at_r], W_RIGHT)
    multiply(right, False)
    arrived(WQ.at[at_f], W_FAR)
    arrived(WK.at[at_f], W_FAR + 1)
    arrived(WV.at[at_f], W_FAR + 2)
    multiply(far, False)
    for gg in range(2):
        for hh in range(2):
            part = ACC[128 * hh:128 * hh + 128, :]
            slot = 2 * gg + hh
            PS[slot, :, 0:256] = part[:, 256 * gg:256 * gg + 256].astype(BF)
            PS[slot, :, 256:384] = part[:, 512 + 128 * gg:640 + 128 * gg].astype(BF)
            PS[slot, :, 384:512] = part[:, 768 + 128 * gg:896 + 128 * gg].astype(BF)

    for d in (2, 1, 3):
        other = up(z, d)
        send(SQ.at[other % 2], SQR.at[d - 1], SQ_IN + d - 1, dev(s, t, other, y))
        send(PS.at[other], PR.at[d - 1], RS_IN + d - 1, dev(s, t, other, y))
    total = PS[z].astype(F32)
    square = SQ[zh]
    rest_of_out_weights()
    for d in (1, 3, 2):
        arrived(SQR.at[d - 1], SQ_IN + d - 1)
        square = square + SQR[d - 1]
        arrived(PR.at[d - 1], RS_IN + d - 1)
        total = total + PR[d - 1].astype(F32)
    inverse_row = lax.rsqrt(square * (1.0 / D) + 1e-5)
    inverse = jnp.transpose(jnp.broadcast_to(inverse_row[0:1], (128, 128)))
    wide = jnp.concatenate([inverse, inverse], axis=1)
    queries = (total[:, 0:256] * wide).astype(BF)
    block = 2 * y + zh
    KV[rows(128 * block, 128), :] = (total[:, 256:512] * wide).astype(BF)

    mine = KV.at[rows(128 * block, 128)]
    for dy in (2, 1, 3, 0):
        for dz in range(2):
            if dy + dz == 0:
                continue
            y_to = up(y, dy)
            h_to = zh if dz == 0 else 1 - zh
            send(mine, mine, KV_IN + 2 * dy + dz - 1, dev(s, t, 2 * g + h_to, y_to), 2 * y_to + h_to > block)

    places = 256 * y + 128 * zh + lax.broadcasted_iota(jnp.int32, (128, 1), 0)
    starts = []
    run = jnp.int32(0)
    for c in range(GROUPS):
        starts.append(run)
        run = run + blocks[c] * UNIT
    lowest = jnp.zeros((128, 1), jnp.int32)
    for c in range(GROUPS - 2):
        lowest = jnp.where(places >= starts[c + 2], starts[c], lowest)
    keys_at = lax.broadcasted_iota(jnp.int32, (128, 1024), 1)
    allowed = (keys_at <= places) & (keys_at >= lowest)

    for dy in (1, 3, 2, 0):
        for dz in range(2):
            if dy + dz == 0:
                continue
            y_from = up(y, 4 - dy)
            h_from = zh if dz == 0 else 1 - zh
            theirs = 2 * y_from + h_from
            arrived(KV.at[rows(128 * theirs, 128)], KV_IN + 2 * dy + dz - 1, theirs < block)

    @pl.when(first)
    def _():
        pl.semaphore_signal(go, inc=1, device_id=dev(1, t, z, y), device_id_type=MESH)

    keys = KV[:, 0:128]
    values = KV[:, 128:256]
    for h in range(2):
        scores = lax.dot_general(
            queries[:, 128 * h:128 * h + 128], keys, (((1,), (1,)), ((), ())), preferred_element_type=F32
        ) * SCALE
        scores = jnp.where(allowed, scores, -jnp.inf)
        exps = jnp.exp(scores - jnp.max(scores, axis=1, keepdims=True))
        norm = jnp.sum(exps, axis=1, keepdims=True)
        heads = jnp.dot(exps.astype(BF), values, preferred_element_type=F32) / norm
        AT[:, 128 * h:128 * h + 128] = heads.astype(BF)

    for d in (2, 1, 3):
        send(AT, ATR.at[z], AT_IN + z, dev(s, up(t, d), t, y))
    send(AT, ATR.at[z], AT_IN + z, dev(s, t, t, y), jnp.logical_not(diagonal))

    @pl.when(diagonal)
    def _():
        ATR[z] = AT[...]
    arrived(WO.at[lower(far)], O_FAR)
    arrived(WO.at[upper(far)], O_FAR + 1)
    for zp in range(4):
        arrived(ATR.at[zp], AT_IN + zp, jnp.logical_not(diagonal & (z == zp)))
    for hh in range(2):
        product = jnp.dot(ATR[hh], WO[0:256, :], preferred_element_type=F32)
        product = product + jnp.dot(ATR[2 + hh], WO[256:512, :], preferred_element_type=F32)
        OS[2 * hh] = product[0:64].astype(BF)
        OS[2 * hh + 1] = product[64:128].astype(BF)
    for d in (2, 1, 3):
        send(OS.at[up(z, d)], OR.at[d - 1], RO_IN + d - 1, dev(s, t, up(z, d), y))
    pl.when(first)(own_res.wait)
    arrived(RES, RES_IN, second)
    state = RES[...].astype(F32)
    projected = OS[z].astype(F32)
    for d in (1, 3, 2):
        arrived(OR.at[d - 1], RO_IN + d - 1)
        projected = projected + OR[d - 1].astype(F32)
    ST[...] = (state + projected).astype(BF)

    my_rows = rows(64 * z, 64)
    for d in (2, 1, 3, 0):
        send(ST, X.at[my_rows], X_IN + z, dev(1, up(t, d), t, y), first)
    send(ST, RES, RES_IN, dev(1, t, z, y), first)

    sec = y // 2
    at_out = rows(256 * (y % 2) + 64 * z, 64)
    ca, cb = pl.ds(0, 512), pl.ds(512, 512)
    keep = second & (sec == 1)

    @pl.when(keep)
    def _():
        FIN[at_out, :] = ST[...]
    cross = second & (sec == 0)
    for d in (2, 1, 3):
        send(ST.at[:, ca], FIN.at[at_out, ca], FA_IN + d, dev(sec, t, up(z, d), y), second)
        send(ST.at[:, cb], FIN.at[at_out, cb], FB_IN + d, dev(sec, t, z, up(y, d)), second)
    send(ST.at[:, ca], FIN.at[at_out, ca], FA_IN, dev(sec, t, z, y), cross)
    send(ST.at[:, cb], FIN.at[at_out, cb], FB_IN, dev(sec, t, z, y), cross)

    holder = sec == s
    for d in (0, 1, 3, 2):
        at = rows(256 * (y % 2) + 64 * up(z, 4 - d), 64)
        arrived(FIN.at[at, ca], FA_IN + d, holder if d else holder & first)
    block_y = rows(256 * (y % 2), 256)
    for d in (2, 1, 3):
        send(FIN.at[block_y, ca], FIN.at[block_y, ca], FAY_IN + d - 1, dev(s, t, z, up(y, d)), holder)
    for d in (0, 1, 3, 2):
        y_from = up(y, 4 - d)
        here = y_from // 2 == s
        at = rows(256 * (y_from % 2) + 64 * z, 64)
        arrived(FIN.at[at, cb], FB_IN + d, here if d else here & first)
    for e in (2, 1, 3):
        for yy in range(2):
            at = rows(256 * yy + 64 * z, 64)
            send(FIN.at[at, cb], FIN.at[at, cb], FBZ_IN + 2 * (e - 1) + yy, dev(s, t, up(z, e), y))
    for d in (1, 3, 2):
        y_from = up(y, 4 - d)
        at = rows(256 * (y_from % 2), 256)
        arrived(FIN.at[at, ca], FAY_IN + d - 1, y_from // 2 == s)
    for e in (1, 3, 2):
        for yy in range(2):
            at = rows(256 * yy + 64 * up(z, 4 - e), 64)
            arrived(FIN.at[at, cb], FBZ_IN + 2 * (e - 1) + yy)
    result = pltpu.make_async_copy(FIN, out, local_sems.at[6])
    result.start()
    for c, when in pending:
        if when is None:
            c.wait_send()
        else:
            pl.when(when)(c.wait_send)
    result.wait()


def on_device(*arrays):
    hbm = pl.BlockSpec(memory_space=pl.ANY)
    vmem = pl.BlockSpec(memory_space=pltpu.VMEM)
    return pl.pallas_call(
        kernel,
        out_shape=jax.ShapeDtypeStruct((512, 1024), BF),
        in_specs=[hbm, vmem, hbm, hbm, hbm, hbm, pl.BlockSpec(memory_space=pltpu.SMEM)],
        out_specs=hbm,
        scratch_shapes=[
            pltpu.VMEM((1024, 512), BF),
            pltpu.VMEM((1024, 256), BF),
            pltpu.VMEM((1024, 256), BF),
            pltpu.VMEM((512, 1024), BF),
            pltpu.VMEM((256, 1024), BF),
            pltpu.VMEM((256, 1024), BF),
            pltpu.VMEM((256, 1024), F32),
            pltpu.VMEM((4, 128, 512), BF),
            pltpu.VMEM((3, 128, 512), BF),
            pltpu.VMEM((2, 8, 128), F32),
            pltpu.VMEM((3, 8, 128), F32),
            pltpu.VMEM((1024, 256), BF),
            pltpu.VMEM((128, 256), BF),
            pltpu.VMEM((4, 128, 256), BF),
            pltpu.VMEM((4, 64, 1024), BF),
            pltpu.VMEM((3, 64, 1024), BF),
            pltpu.VMEM((64, 1024), BF),
            pltpu.VMEM((64, 1024), BF),
            pltpu.VMEM((512, 1024), BF),
            pltpu.SemaphoreType.DMA((N_SEND,)),
            pltpu.SemaphoreType.DMA((N_RECV,)),
            pltpu.SemaphoreType.DMA((N_LOCAL,)),
            pltpu.SemaphoreType.REGULAR,
        ],
        compiler_params=pltpu.CompilerParams(
            collective_id=0, has_side_effects=True, vmem_limit_bytes=56 * 1024 * 1024
        ),
    )(*arrays)


def solution(mesh):
    in_specs = (
        P(None, "tp"),
        P("section", None),
        P("section", "rep", "tp"),
        P("section", "rep", "tp"),
        P("section", "rep", "tp"),
        P("section", "rep", "tp"),
        P(),
    )
    return jax.shard_map(
        on_device, mesh=mesh, in_specs=in_specs, out_specs=P("section", "tp"), check_vma=False
    )
```

time: 1260 us -> 92.9 us (0.07)
  waiting for transfers between devices: 481 us -> 0 us
  blocking collectives: 468 us -> 0 us
  local copies, waits for them, and re-layouts: 113 us -> 2.26 us
  Pallas kernels: 0 us -> 90.4 us
  matrix products: 82.8 us -> 0 us
  other arithmetic: 58.8 us -> 0 us
  loops' own time: 24.7 us -> 0 us
  between operations: 13.6 us -> 0.01 us
    all_gather x36 -> x0, blocking collectives: 468 us -> none  [the longest x9 158 us: one_tick(): lax.all_gather(value_rows, 'rep', axis=0, tiled=True)]
    all_gather x5 -> x0, waiting for transfers between devices: 306 us -> none  [the longest x1 112 us: on_device(): both_halves = lax.all_gather(mine, 'rep', axis=1, tiled=True)]
    ppermute x9 -> x0, waiting for transfers between devices: 146 us -> none  [from_behind(): return lax.ppermute(block, axis, route)]
    pallas_call x0 -> x1, Pallas kernels: none -> 90.4 us  [on_device(): pl.pallas_call(kernel, out_shape=jax.ShapeDtypeStruct((512, 1024), BF), i...]
    dot_general x48 -> x0, matrix products: 82.8 us -> none  [the longest x8 27.8 us: product(): return jnp.dot(received, w_out, preferred_element_type=jnp.float32)]
    dynamic_update_slice x27 -> x0, local copies, waits for them, and re-layouts: 38.8 us -> none  [the longest x9 15.6 us: one_tick(): lax.dynamic_update_slice_in_dim(value_cache, jnp.where(working, block_val...]
    psum x1 -> x0, waiting for transfers between devices: 25.8 us -> none  [broadcast(): return lax.psum(kept, axis)]
    select_n x38 -> x0, other arithmetic: 25.4 us -> none  [the longest x9 8.03 us: one_tick(): jnp.where(working, updated, old_rows)]
  transfers between devices with their start and end apart: 15 -> 0, of which waited for: 15 -> 0; matrix products, arithmetic and copies ran while one was open for 2% -> 0% of each run, Pallas kernels for 0% -> 0%
where the time goes in v1:
time: 92.9 us; the launch traced here: 92.7 us
  Pallas kernels  90.4 us (97%)
  local copies, waits for them, and re-layouts  2.26 us (2%)
    pallas_call x1, Pallas kernels, on_device(): pl.pallas_call(kernel, out_shape=jax.ShapeDtypeStruct((512, 1024), BF), i...  90.4 us
    unnamed x1, local copies, waits for them, and re-layouts  2.26 us

profile of v1, /device:TPU:1, one launch (start us, length us, event | category | flops | bytes accessed | tf_op | source)
XLA Modules:
  0.0 92.7 jit_solution(9300585439222423997)
XLA Ops:
  0.0 90.4 %shard_map.73 = bf16[512,1024]{1,0:T(8,128)(2,1)} custom-call(bf16[1024,1024]{1,0:T(8,128)(2,1)} %emb.1, f32[1,4096]{1,0:T(1,128)} %gain.1, bf16[1,256,512]{2,1,0:T(8,128)(2,1)} %wq.1, bf16[1,256,256]{2,1,0:T(8,128)(2,1)} %wk.1, bf16[1,256,256]{2,1,0:T(8,128)(2,1)} %wv.1, bf16[1,128,1024]{2,1,0:T(8,128)(2,1)} %wo.1, s32[8]{0:T(128)} %blocks.1), custom_call_target="tpu_custom_call" | custom-call | tf_op jit(solution)/shard_map/pallas_call | solution.py:376
  90.5 2.3 %copy.9 = bf16[512,1024]{1,0:T(8,128)(2,1)} copy(bf16[512,1024]{1,0:T(8,128)(2,1)} %shard_map.73) | data formatting | bytes 2097152

commit v2 on v1

v2 whole, which is shorter than its diff:
```python
import math

import jax
import jax.numpy as jnp
from jax import lax
from jax.experimental import pallas as pl
from jax.experimental.pallas import tpu as pltpu
from jax.sharding import PartitionSpec as P

MESH = pl.DeviceIdType.MESH
BF = jnp.bfloat16
F32 = jnp.float32
D = 4096
GROUPS = 8
UNIT = 16
SCALE = 1.0 / math.sqrt(128)

KV_LEFT, KV_RIGHT, KV_FAR = 0, 2, 4
Q_LEFT, Q_RIGHT, Q_FAR = 6, 8, 10
O_LEFT, O_RIGHT, O_FAR = 12, 13, 14
X_IN = 16
RS_IN, SQ_IN, RQ_IN = 24, 27, 30
KV_IN = 33
AT_IN = 40
RO_IN = 44
RES_IN = 50
FIN_IN = 52
N_RECV = 84
N_SEND = 128
N_LOCAL = 8


def kernel(
    emb, gain, wq, wk, wv, wo, blocks, out,
    WKV, WQ, WO, X, XG, PK, PKR, PQ, PQR, SQ, SQR, KV, AT, ATR, OS, OR, RES, ST,
    send_sems, recv_sems, local_sems, go,
):
    s = lax.axis_index("section")
    t = lax.axis_index("tp")
    r = lax.axis_index("rep")
    z = r // 4
    y = r % 4
    g = z // 2
    zh = z % 2
    first = s == 0
    second = s == 1
    diagonal = z == t
    apart = jnp.logical_not(diagonal)

    def dev(s_, t_, z_, y_):
        return (s_, t_, z_ * 4 + y_)

    def up(v, d):
        return (v + d) % 4

    pending = []

    def send(src, dst, ridx, device, when=None):
        c = pltpu.make_async_remote_copy(
            src_ref=src, dst_ref=dst, send_sem=send_sems.at[len(pending)],
            recv_sem=recv_sems.at[ridx], device_id=device, device_id_type=MESH,
        )
        if when is None:
            c.start()
        else:
            pl.when(when)(c.start)
        pending.append((c, when))

    def arrived(ref, ridx, when=None):
        c = pltpu.make_async_remote_copy(
            src_ref=ref, dst_ref=ref, send_sem=send_sems.at[0],
            recv_sem=recv_sems.at[ridx], device_id=dev(1 - s, t, z, y), device_id_type=MESH,
        )
        if when is None:
            c.wait_recv()
        else:
            pl.when(when)(c.wait_recv)

    def rows(start, size):
        return pl.ds(pl.multiple_of(start, size), size)

    KV[...] = jnp.zeros_like(KV)

    at_y = rows(256 * y, 256)
    kc, vc = pl.ds(0, 256), pl.ds(256, 256)
    own = [
        pltpu.make_async_copy(wk.at[0], WKV.at[at_y, kc], local_sems.at[0]),
        pltpu.make_async_copy(wv.at[0], WKV.at[at_y, vc], local_sems.at[1]),
        pltpu.make_async_copy(wq.at[0], WQ.at[at_y], local_sems.at[2]),
        pltpu.make_async_copy(wo.at[0], WO.at[rows(128 * y, 128)], local_sems.at[3]),
    ]
    for c in own:
        c.start()
    my_emb = emb.at[rows(256 * y + 64 * z, 64)]
    my_rows = rows(64 * z, 64)
    own_x = pltpu.make_async_copy(my_emb, X.at[my_rows], local_sems.at[4])
    own_res = pltpu.make_async_copy(my_emb, RES, local_sems.at[5])
    pl.when(first & diagonal)(own_x.start)
    pl.when(first)(own_res.start)

    barrier = pltpu.get_barrier_semaphore()

    def greet(device):
        pl.semaphore_signal(barrier, inc=1, device_id=device, device_id_type=MESH)

    for d in (1, 2, 3):
        greet(dev(s, t, z, up(y, d)))
        greet(dev(s, t, up(z, d), y))
        greet(dev(s, t, z + 1 - 2 * zh, up(y, d)))
        greet(dev(1 - s, t, z, up(y, d)))
        greet(dev(1 - s, t, up(z, d), y))
        greet(dev(s, up(t, d), t, y))
        greet(dev(s, z, up(z, d), y))
    greet(dev(1 - s, t, z, y))

    @pl.when(apart)
    def _():
        greet(dev(s, t, t, y))
        greet(dev(s, z, z, y))

    for d in range(4):
        @pl.when(first)
        def _():
            greet(dev(1, d, t, y))

        @pl.when(second)
        def _():
            greet(dev(0, z, d, y))
    pl.semaphore_wait(barrier, 26 + 2 * (1 - diagonal.astype(jnp.int32)))

    right, left, far = up(y, 1), up(y, 3), up(y, 2)
    dev_r, dev_l = dev(s, t, z, right), dev(s, t, z, left)
    at_l, at_r, at_f = rows(256 * left, 256), rows(256 * right, 256), rows(256 * far, 256)

    half = (pl.ds(0, 512), pl.ds(512, 512))
    for d in (2, 1, 3):
        send(my_emb, X.at[my_rows], X_IN + z, dev(0, up(t, d), t, y), first)
    send(my_emb, X.at[my_rows], X_IN + z, dev(0, t, t, y), first & apart)

    @pl.when(second)
    def _():
        pl.semaphore_wait(go, 1)

    send(wk.at[0], WKV.at[at_y, kc], KV_LEFT, dev_r)
    send(wv.at[0], WKV.at[at_y, vc], KV_RIGHT + 1, dev_l)
    send(wv.at[0], WKV.at[at_y, vc], KV_LEFT + 1, dev_r)
    send(wk.at[0], WKV.at[at_y, kc], KV_RIGHT, dev_l)
    arrived(WKV.at[at_l, kc], KV_LEFT)
    send(WKV.at[at_l, kc], WKV.at[at_l, kc], KV_FAR, dev_r)
    arrived(WKV.at[at_r, vc], KV_RIGHT + 1)
    send(WKV.at[at_r, vc], WKV.at[at_r, vc], KV_FAR + 1, dev_l)

    def q_rows(block, h):
        return rows(256 * block + 128 * h, 128)

    q_src = (wq.at[0, pl.ds(0, 128)], wq.at[0, pl.ds(128, 128)])
    send(q_src[0], WQ.at[q_rows(y, 0)], Q_LEFT, dev_r)
    send(q_src[1], WQ.at[q_rows(y, 1)], Q_RIGHT + 1, dev_l)
    send(q_src[1], WQ.at[q_rows(y, 1)], Q_LEFT + 1, dev_r)
    send(q_src[0], WQ.at[q_rows(y, 0)], Q_RIGHT, dev_l)

    def forward_q(when):
        low, high = WQ.at[q_rows(left, 0)], WQ.at[q_rows(right, 1)]
        arrived(low, Q_LEFT, when)
        send(low, low, Q_FAR, dev_r, when)
        arrived(high, Q_RIGHT + 1, when)
        send(high, high, Q_FAR + 1, dev_l, when)

    ow_y = rows(128 * y, 128)
    ow_l, ow_r = rows(128 * left, 128), rows(128 * right, 128)

    def out_part(block, h):
        return WO.at[rows(128 * block + 64 * h, 64)]

    def send_out_weights(when):
        send(wo.at[0], WO.at[ow_y], O_LEFT, dev_r, when)
        send(wo.at[0], WO.at[ow_y], O_RIGHT, dev_l, when)

    def forward_out_weights(when):
        arrived(WO.at[ow_l], O_LEFT, when)
        send(out_part(left, 0), out_part(left, 0), O_FAR, dev_r, when)
        arrived(WO.at[ow_r], O_RIGHT, when)
        send(out_part(right, 1), out_part(right, 1), O_FAR + 1, dev_l, when)

    forward_q(second)
    send_out_weights(second)
    forward_out_weights(second)

    pl.when(first & diagonal)(own_x.wait)
    for zp in range(4):
        place = pl.ds(64 * zp, 64)
        arrived(X.at[place], X_IN + zp, first & jnp.logical_not(diagonal & (z == zp)))
    for c in range(2):
        for zp in range(4):
            arrived(X.at[pl.ds(64 * zp, 64), half[c]], X_IN + 4 * c + zp, second)
    x = X[...].astype(F32)
    XG[...] = (x * gain[:, rows(1024 * z, 1024)]).astype(BF)
    squares = jnp.sum(x * x, axis=1, keepdims=True)
    for h in range(2):
        column = jnp.broadcast_to(squares[128 * h:128 * h + 128], (128, 128))
        SQ[h] = jnp.transpose(column)[0:8]
    for d in (2, 1, 3):
        other = up(z, d)
        send(SQ.at[other % 2], SQR.at[d - 1], SQ_IN + d - 1, dev(s, t, other, y))

    def multiply(block, ref):
        at = rows(256 * block, 256)
        return jnp.dot(XG[:, at], ref[at, :], preferred_element_type=F32)

    for c in own:
        c.wait()
    part = multiply(y, WKV)
    arrived(WKV.at[at_l, vc], KV_LEFT + 1)
    part = part + multiply(left, WKV)
    arrived(WKV.at[at_r, kc], KV_RIGHT)
    part = part + multiply(right, WKV)
    arrived(WKV.at[at_f, kc], KV_FAR)
    arrived(WKV.at[at_f, vc], KV_FAR + 1)
    part = part + multiply(far, WKV)
    for gg in range(2):
        for hh in range(2):
            rows_of = part[128 * hh:128 * hh + 128]
            PK[2 * gg + hh, :, 0:128] = rows_of[:, 128 * gg:128 * gg + 128].astype(BF)
            PK[2 * gg + hh, :, 128:256] = rows_of[:, 256 + 128 * gg:384 + 128 * gg].astype(BF)
    for d in (2, 1, 3):
        other = up(z, d)
        send(PK.at[other], PKR.at[d - 1], RS_IN + d - 1, dev(s, t, other, y))

    forward_q(first)
    part = multiply(y, WQ)
    arrived(WQ.at[q_rows(left, 1)], Q_LEFT + 1)
    part = part + multiply(left, WQ)
    arrived(WQ.at[q_rows(right, 0)], Q_RIGHT)
    part = part + multiply(right, WQ)
    arrived(WQ.at[q_rows(far, 0)], Q_FAR)
    arrived(WQ.at[q_rows(far, 1)], Q_FAR + 1)
    part = part + multiply(far, WQ)
    for gg in range(2):
        for hh in range(2):
            PQ[2 * gg + hh] = part[128 * hh:128 * hh + 128, 256 * gg:256 * gg + 256].astype(BF)
    for d in (2, 1, 3):
        other = up(z, d)
        send(PQ.at[other], PQR.at[d - 1], RQ_IN + d - 1, dev(s, t, other, y))

    square = SQ[zh]
    for d in (1, 3, 2):
        arrived(SQR.at[d - 1], SQ_IN + d - 1)
        square = square + SQR[d - 1]
    inverse_row = lax.rsqrt(square * (1.0 / D) + 1e-5)
    inverse = jnp.transpose(jnp.broadcast_to(inverse_row[0:1], (128, 128)))
    wide = jnp.concatenate([inverse, inverse], axis=1)
    total = PK[z].astype(F32)
    for d in (1, 3, 2):
        arrived(PKR.at[d - 1], RS_IN + d - 1)
        total = total + PKR[d - 1].astype(F32)
    block = 2 * y + zh
    KV[rows(128 * block, 128), :] = (total * wide).astype(BF)
    mine = KV.at[rows(128 * block, 128)]
    for dy in (2, 1, 3, 0):
        for dz in range(2):
            if dy + dz == 0:
                continue
            y_to = up(y, dy)
            h_to = zh if dz == 0 else 1 - zh
            send(mine, mine, KV_IN + 2 * dy + dz - 1, dev(s, t, 2 * g + h_to, y_to), 2 * y_to + h_to > block)
    send_out_weights(first)

    places = 256 * y + 128 * zh + lax.broadcasted_iota(jnp.int32, (128, 1), 0)
    starts = []
    run = jnp.int32(0)
    for c in range(GROUPS):
        starts.append(run)
        run = run + blocks[c] * UNIT
    lowest = jnp.zeros((128, 1), jnp.int32)
    for c in range(GROUPS - 2):
        lowest = jnp.where(places >= starts[c + 2], starts[c], lowest)
    keys_at = lax.broadcasted_iota(jnp.int32, (128, 1024), 1)
    allowed = (keys_at <= places) & (keys_at >= lowest)

    total = PQ[z].astype(F32)
    for d in (1, 3, 2):
        arrived(PQR.at[d - 1], RQ_IN + d - 1)
        total = total + PQR[d - 1].astype(F32)
    queries = (total * wide).astype(BF)

    for dy in (1, 3, 2, 0):
        for dz in range(2):
            if dy + dz == 0:
                continue
            y_from = up(y, 4 - dy)
            h_from = zh if dz == 0 else 1 - zh
            theirs = 2 * y_from + h_from
            arrived(KV.at[rows(128 * theirs, 128)], KV_IN + 2 * dy + dz - 1, theirs < block)

    keys = KV[:, 0:128]
    values = KV[:, 128:256]
    for h in range(2):
        scores = lax.dot_general(
            queries[:, 128 * h:128 * h + 128], keys, (((1,), (1,)), ((), ())), preferred_element_type=F32
        ) * SCALE
        scores = jnp.where(allowed, scores, -jnp.inf)
        exps = jnp.exp(scores - jnp.max(scores, axis=1, keepdims=True))
        norm = jnp.sum(exps, axis=1, keepdims=True)
        heads = jnp.dot(exps.astype(BF), values, preferred_element_type=F32) / norm
        AT[:, 128 * h:128 * h + 128] = heads.astype(BF)

    for d in (2, 1, 3):
        send(AT, ATR.at[z], AT_IN + z, dev(s, up(t, d), t, y))
    send(AT, ATR.at[z], AT_IN + z, dev(s, t, t, y), apart)

    @pl.when(diagonal)
    def _():
        ATR[z] = AT[...]

    forward_out_weights(first)

    @pl.when(first)
    def _():
        pl.semaphore_signal(go, inc=1, device_id=dev(1, t, z, y), device_id_type=MESH)

    pl.when(first)(own_res.wait)
    for c in range(2):
        arrived(RES.at[:, half[c]], RES_IN + c, second)
    arrived(out_part(far, 0), O_FAR)
    arrived(out_part(far, 1), O_FAR + 1)
    for zp in range(4):
        arrived(ATR.at[zp], AT_IN + zp, jnp.logical_not(diagonal & (z == zp)))
    for c in range(2):
        for hh in range(2):
            product = jnp.dot(ATR[hh], WO[0:256, half[c]], preferred_element_type=F32)
            product = product + jnp.dot(ATR[2 + hh], WO[256:512, half[c]], preferred_element_type=F32)
            OS[c, 2 * hh] = product[0:64].astype(BF)
            OS[c, 2 * hh + 1] = product[64:128].astype(BF)
        for d in (2, 1, 3):
            send(OS.at[c, up(z, d)], OR.at[c, d - 1], RO_IN + 3 * c + d - 1, dev(s, t, up(z, d), y))

    sec = y // 2
    cross = second & (sec == 0)

    def out_rows(z_, y_):
        return rows(256 * (y_ % 2) + 64 * z_, 64)

    at_out = out_rows(z, y)

    def fin(c, dz, dy):
        return FIN_IN + 16 * c + 4 * dz + dy

    for c in range(2):
        new = RES[:, half[c]].astype(F32) + OS[c, z].astype(F32)
        for d in (1, 3, 2):
            arrived(OR.at[c, d - 1], RO_IN + 3 * c + d - 1)
            new = new + OR[c, d - 1].astype(F32)
        ST[:, half[c]] = new.astype(BF)
        mine = ST.at[:, half[c]]
        for d in (2, 1, 3, 0):
            send(mine, X.at[my_rows, half[c]], X_IN + 4 * c + z, dev(1, up(t, d), t, y), first)
        send(mine, RES.at[:, half[c]], RES_IN + c, dev(1, t, z, y), first)
        place = out.at[at_out, half[c]]
        for d in (2, 1, 3):
            send(mine, place, fin(c, d, 0), dev(sec, t, up(z, d), y), second)
            send(mine, place, fin(c, 0, d), dev(sec, t, z, up(y, d)), second)
        send(mine, place, fin(c, 0, 0), dev(sec, t, z, y), cross)

    @pl.when(second & (sec == 1))
    def _():
        out[at_out, :] = ST[...]

    holder = sec == s
    for d in (1, 3, 2):
        place = out.at[out_rows(up(z, 4 - d), y), half[0]]
        arrived(place, fin(0, d, 0), holder)
        for e in (2, 1, 3):
            send(place, place, fin(0, d, e), dev(s, t, z, up(y, e)), holder)
        y_from = up(y, 4 - d)
        here = y_from // 2 == s
        place = out.at[out_rows(z, y_from), half[1]]
        arrived(place, fin(1, 0, d), here)
        for e in (2, 1, 3):
            send(place, place, fin(1, e, d), dev(s, t, up(z, e), y), here)
    for c in range(2):
        arrived(out.at[at_out, half[c]], fin(c, 0, 0), holder & first)
    for d in (1, 3, 2):
        y_from = up(y, 4 - d)
        arrived(out.at[out_rows(z, y_from), half[0]], fin(0, 0, d), y_from // 2 == s)
        arrived(out.at[out_rows(up(z, 4 - d), y), half[1]], fin(1, d, 0), holder)
    for e in (1, 3, 2):
        for d in (1, 3, 2):
            y_from = up(y, 4 - d)
            z_from = up(z, 4 - e)
            for c in range(2):
                arrived(out.at[out_rows(z_from, y_from), half[c]], fin(c, e, d), y_from // 2 == s)
    for c, when in pending:
        if when is None:
            c.wait_send()
        else:
            pl.when(when)(c.wait_send)


def on_device(*arrays):
    hbm = pl.BlockSpec(memory_space=pl.ANY)
    vmem = pl.BlockSpec(memory_space=pltpu.VMEM)
    return pl.pallas_call(
        kernel,
        out_shape=pltpu.VMEM((512, 1024), BF),
        in_specs=[hbm, vmem, hbm, hbm, hbm, hbm, pl.BlockSpec(memory_space=pltpu.SMEM)],
        out_specs=vmem,
        scratch_shapes=[
            pltpu.VMEM((1024, 512), BF),
            pltpu.VMEM((1024, 512), BF),
            pltpu.VMEM((512, 1024), BF),
            pltpu.VMEM((256, 1024), BF),
            pltpu.VMEM((256, 1024), BF),
            pltpu.VMEM((4, 128, 256), BF),
            pltpu.VMEM((3, 128, 256), BF),
            pltpu.VMEM((4, 128, 256), BF),
            pltpu.VMEM((3, 128, 256), BF),
            pltpu.VMEM((2, 8, 128), F32),
            pltpu.VMEM((3, 8, 128), F32),
            pltpu.VMEM((1024, 256), BF),
            pltpu.VMEM((128, 256), BF),
            pltpu.VMEM((4, 128, 256), BF),
            pltpu.VMEM((2, 4, 64, 512), BF),
            pltpu.VMEM((2, 3, 64, 512), BF),
            pltpu.VMEM((64, 1024), BF),
            pltpu.VMEM((64, 1024), BF),
            pltpu.SemaphoreType.DMA((N_SEND,)),
            pltpu.SemaphoreType.DMA((N_RECV,)),
            pltpu.SemaphoreType.DMA((N_LOCAL,)),
            pltpu.SemaphoreType.REGULAR,
        ],
        compiler_params=pltpu.CompilerParams(
            collective_id=0, has_side_effects=True, vmem_limit_bytes=56 * 1024 * 1024
        ),
    )(*arrays)


def solution(mesh):
    in_specs = (
        P(None, "tp"),
        P("section", None),
        P("section", "rep", "tp"),
        P("section", "rep", "tp"),
        P("section", "rep", "tp"),
        P("section", "rep", "tp"),
        P(),
    )
    return jax.shard_map(
        on_device, mesh=mesh, in_specs=in_specs, out_specs=P("section", "tp"), check_vma=False
    )
```

time: 92.9 us -> 82.5 us (0.89)
  Pallas kernels: 90.4 us -> 81.3 us
  local copies, waits for them, and re-layouts: 2.26 us -> 0.97 us
    pallas_call x1, Pallas kernels: 90.4 us -> 81.3 us  [on_device(): pl.pallas_call(kernel, out_shape=pltpu.VMEM((512, 1024), BF), in_specs=[h...]
    unnamed x1, local copies, waits for them, and re-layouts: 2.26 us -> 0.97 us
where the time goes in v2:
time: 82.5 us; the launch traced here: 82.3 us
  Pallas kernels  81.3 us (99%)
  local copies, waits for them, and re-layouts  0.97 us (1%)
    pallas_call x1, Pallas kernels, on_device(): pl.pallas_call(kernel, out_shape=pltpu.VMEM((512, 1024), BF), in_specs=[h...  81.3 us

profile of v2, /device:TPU:1, one launch (start us, length us, event | category | flops | bytes accessed | tf_op | source)
XLA Modules:
  0.0 82.3 jit_solution(14629864513121397595)
XLA Ops:
  0.0 81.3 %shard_map.73 = bf16[512,1024]{1,0:T(8,128)(2,1)S(1)} custom-call(bf16[1024,1024]{1,0:T(8,128)(2,1)} %emb.1, f32[1,4096]{1,0:T(1,128)} %gain.1, bf16[1,256,512]{2,1,0:T(8,128)(2,1)} %wq.1, bf16[1,256,256]{2,1,0:T(8,128)(2,1)} %wk.1, bf16[1,256,256]{2,1,0:T(8,128)(2,1)} %wv.1, bf16[1,128,1024]{2,1,0:T(8,128)(2,1)} %wo.1, s32[8]{0:T(128)} %blocks.1), custom_call_target="tpu_custom_call" | custom-call | tf_op jit(solution)/shard_map/pallas_call | solution.py:402
  81.3 1.0 %copy.9 = bf16[512,1024]{1,0:T(8,128)(2,1)} copy(bf16[512,1024]{1,0:T(8,128)(2,1)S(1)} %shard_map.73) | data formatting | bytes 2097152

commit v3 on v2

--- a/solution.py
+++ b/solution.py
@@ -22,17 +22,17 @@
 RS_IN, SQ_IN, RQ_IN = 24, 27, 30
 KV_IN = 33
 AT_IN = 40
-RO_IN = 44
-RES_IN = 50
-FIN_IN = 52
-N_RECV = 84
-N_SEND = 128
+RO_IN = 48
+RES_IN = 54
+FIN_IN = 56
+N_RECV = 88
+N_SEND = 136
 N_LOCAL = 8
 
 
 def kernel(
     emb, gain, wq, wk, wv, wo, blocks, out,
-    WKV, WQ, WO, X, XG, PK, PKR, PQ, PQR, SQ, SQR, KV, AT, ATR, OS, OR, RES, ST,
+    WKV, WQ, WO, X, XG, PK, PKR, PQ, PQR, SQ, SQR, KV, AT, ATR, OS, OR, RES, ST, GAIN,
     send_sems, recv_sems, local_sems, go,
 ):
     s = lax.axis_index("section")
@@ -66,6 +66,16 @@
             pl.when(when)(c.start)
         pending.append((c, when))
 
+    finished = [0]
+
+    def flush(count):
+        for c, when in pending[finished[0]:count]:
+            if when is None:
+                c.wait_send()
+            else:
+                pl.when(when)(c.wait_send)
+        finished[0] = max(finished[0], count)
+
     def arrived(ref, ridx, when=None):
         c = pltpu.make_async_remote_copy(
             src_ref=ref, dst_ref=ref, send_sem=send_sems.at[0],
@@ -81,6 +91,34 @@
 
     KV[...] = jnp.zeros_like(KV)
 
+    barrier = pltpu.get_barrier_semaphore()
+
+    def greet(device):
+        pl.semaphore_signal(barrier, inc=1, device_id=device, device_id_type=MESH)
+
+    for d in (1, 2, 3):
+        greet(dev(s, t, z, up(y, d)))
+        greet(dev(s, t, up(z, d), y))
+        greet(dev(s, t, z + 1 - 2 * zh, up(y, d)))
+        greet(dev(1 - s, t, z, up(y, d)))
+        greet(dev(1 - s, t, up(z, d), y))
+        greet(dev(s, up(t, d), t, y))
+        greet(dev(s, z, up(z, d), y))
+    greet(dev(1 - s, t, z, y))
+
+    @pl.when(apart)
+    def _():
+        greet(dev(s, t, t, y))
+        greet(dev(s, z, z, y))
+
+    for d in range(4):
+        @pl.when(first)
+        def _():
+            greet(dev(1, d, t, y))
+
+        @pl.when(second)
+        def _():
+            greet(dev(0, z, d, y))
     at_y = rows(256 * y, 256)
     kc, vc = pl.ds(0, 256), pl.ds(256, 256)
     own = [
@@ -88,6 +126,7 @@
         pltpu.make_async_copy(wv.at[0], WKV.at[at_y, vc], local_sems.at[1]),
         pltpu.make_async_copy(wq.at[0], WQ.at[at_y], local_sems.at[2]),
         pltpu.make_async_copy(wo.at[0], WO.at[rows(128 * y, 128)], local_sems.at[3]),
+        pltpu.make_async_copy(gain, GAIN, local_sems.at[6]),
     ]
     for c in own:
         c.start()
@@ -98,34 +137,6 @@
     pl.when(first & diagonal)(own_x.start)
     pl.when(first)(own_res.start)
 
-    barrier = pltpu.get_barrier_semaphore()
-
-    def greet(device):
-        pl.semaphore_signal(barrier, inc=1, device_id=device, device_id_type=MESH)
-
-    for d in (1, 2, 3):
-        greet(dev(s, t, z, up(y, d)))
-        greet(dev(s, t, up(z, d), y))
-        greet(dev(s, t, z + 1 - 2 * zh, up(y, d)))
-        greet(dev(1 - s, t, z, up(y, d)))
-        greet(dev(1 - s, t, up(z, d), y))
-        greet(dev(s, up(t, d), t, y))
-        greet(dev(s, z, up(z, d), y))
-    greet(dev(1 - s, t, z, y))
-
-    @pl.when(apart)
-    def _():
-        greet(dev(s, t, t, y))
-        greet(dev(s, z, z, y))
-
-    for d in range(4):
-        @pl.when(first)
-        def _():
-            greet(dev(1, d, t, y))
-
-        @pl.when(second)
-        def _():
-            greet(dev(0, z, d, y))
     pl.semaphore_wait(barrier, 26 + 2 * (1 - diagonal.astype(jnp.int32)))
 
     right, left, far = up(y, 1), up(y, 3), up(y, 2)
@@ -193,22 +204,14 @@
     for c in range(2):
         for zp in range(4):
             arrived(X.at[pl.ds(64 * zp, 64), half[c]], X_IN + 4 * c + zp, second)
+    for c in own:
+        c.wait()
     x = X[...].astype(F32)
-    XG[...] = (x * gain[:, rows(1024 * z, 1024)]).astype(BF)
-    squares = jnp.sum(x * x, axis=1, keepdims=True)
-    for h in range(2):
-        column = jnp.broadcast_to(squares[128 * h:128 * h + 128], (128, 128))
-        SQ[h] = jnp.transpose(column)[0:8]
-    for d in (2, 1, 3):
-        other = up(z, d)
-        send(SQ.at[other % 2], SQR.at[d - 1], SQ_IN + d - 1, dev(s, t, other, y))
-
+    XG[...] = (x * GAIN[:, rows(1024 * z, 1024)]).astype(BF)
     def multiply(block, ref):
         at = rows(256 * block, 256)
         return jnp.dot(XG[:, at], ref[at, :], preferred_element_type=F32)
 
-    for c in own:
-        c.wait()
     part = multiply(y, WKV)
     arrived(WKV.at[at_l, vc], KV_LEFT + 1)
     part = part + multiply(left, WKV)
@@ -227,6 +230,15 @@
         send(PK.at[other], PKR.at[d - 1], RS_IN + d - 1, dev(s, t, other, y))
 
     forward_q(first)
+    send_out_weights(first)
+    squares = jnp.sum(x * x, axis=1, keepdims=True)
+    for h in range(2):
+        column = jnp.broadcast_to(squares[128 * h:128 * h + 128], (128, 128))
+        SQ[h] = jnp.transpose(column)[0:8]
+    for d in (2, 1, 3):
+        other = up(z, d)
+        send(SQ.at[other % 2], SQR.at[d - 1], SQ_IN + d - 1, dev(s, t, other, y))
+
     part = multiply(y, WQ)
     arrived(WQ.at[q_rows(left, 1)], Q_LEFT + 1)
     part = part + multiply(left, WQ)
@@ -263,7 +275,7 @@
             y_to = up(y, dy)
             h_to = zh if dz == 0 else 1 - zh
             send(mine, mine, KV_IN + 2 * dy + dz - 1, dev(s, t, 2 * g + h_to, y_to), 2 * y_to + h_to > block)
-    send_out_weights(first)
+    front = len(pending)
 
     places = 256 * y + 128 * zh + lax.broadcasted_iota(jnp.int32, (128, 1), 0)
     starts = []
@@ -277,6 +289,7 @@
     keys_at = lax.broadcasted_iota(jnp.int32, (128, 1024), 1)
     allowed = (keys_at <= places) & (keys_at >= lowest)
 
+    forward_out_weights(first)
     total = PQ[z].astype(F32)
     for d in (1, 3, 2):
         arrived(PQR.at[d - 1], RQ_IN + d - 1)
@@ -302,17 +315,16 @@
         exps = jnp.exp(scores - jnp.max(scores, axis=1, keepdims=True))
         norm = jnp.sum(exps, axis=1, keepdims=True)
         heads = jnp.dot(exps.astype(BF), values, preferred_element_type=F32) / norm
-        AT[:, 128 * h:128 * h + 128] = heads.astype(BF)
-
-    for d in (2, 1, 3):
-        send(AT, ATR.at[z], AT_IN + z, dev(s, up(t, d), t, y))
-    send(AT, ATR.at[z], AT_IN + z, dev(s, t, t, y), apart)
+        AT[h] = heads.astype(BF)
+        for d in (2, 1, 3):
+            send(AT.at[h], ATR.at[z, h], AT_IN + 4 * h + z, dev(s, up(t, d), t, y))
+        send(AT.at[h], ATR.at[z, h], AT_IN + 4 * h + z, dev(s, t, t, y), apart)
 
     @pl.when(diagonal)
     def _():
         ATR[z] = AT[...]
 
-    forward_out_weights(first)
+    flush(front)
 
     @pl.when(first)
     def _():
@@ -324,15 +336,21 @@
     arrived(out_part(far, 0), O_FAR)
     arrived(out_part(far, 1), O_FAR + 1)
     for zp in range(4):
-        arrived(ATR.at[zp], AT_IN + zp, jnp.logical_not(diagonal & (z == zp)))
+        for h in range(2):
+            arrived(ATR.at[zp, h], AT_IN + 4 * h + zp, jnp.logical_not(diagonal & (z == zp)))
     for c in range(2):
         for hh in range(2):
-            product = jnp.dot(ATR[hh], WO[0:256, half[c]], preferred_element_type=F32)
-            product = product + jnp.dot(ATR[2 + hh], WO[256:512, half[c]], preferred_element_type=F32)
+            product = jnp.zeros((128, 512), F32)
+            for q in range(4):
+                product = product + jnp.dot(
+                    ATR[2 * (q // 2) + hh, q % 2], WO[128 * q:128 * q + 128, half[c]], preferred_element_type=F32
+                )
             OS[c, 2 * hh] = product[0:64].astype(BF)
             OS[c, 2 * hh + 1] = product[64:128].astype(BF)
         for d in (2, 1, 3):
             send(OS.at[c, up(z, d)], OR.at[c, d - 1], RO_IN + 3 * c + d - 1, dev(s, t, up(z, d), y))
+
+    summed = len(pending)
 
     sec = y // 2
     cross = second & (sec == 0)
@@ -357,8 +375,17 @@
         send(mine, RES.at[:, half[c]], RES_IN + c, dev(1, t, z, y), first)
         place = out.at[at_out, half[c]]
         for d in (2, 1, 3):
-            send(mine, place, fin(c, d, 0), dev(sec, t, up(z, d), y), second)
-            send(mine, place, fin(c, 0, d), dev(sec, t, z, up(y, d)), second)
+            if c == 0:
+                send(mine, place, fin(c, d, 0), dev(sec, t, up(z, d), y), second)
+            else:
+                send(mine, place, fin(c, 0, d), dev(sec, t, z, up(y, d)), second)
+    for c in range(2):
+        mine, place = ST.at[:, half[c]], out.at[at_out, half[c]]
+        for d in (2, 1, 3):
+            if c == 0:
+                send(mine, place, fin(c, 0, d), dev(sec, t, z, up(y, d)), second)
+            else:
+                send(mine, place, fin(c, d, 0), dev(sec, t, up(z, d), y), second)
         send(mine, place, fin(c, 0, 0), dev(sec, t, z, y), cross)
 
     @pl.when(second & (sec == 1))
@@ -377,6 +404,7 @@
         arrived(place, fin(1, 0, d), here)
         for e in (2, 1, 3):
             send(place, place, fin(1, e, d), dev(s, t, up(z, e), y), here)
+    flush(summed)
     for c in range(2):
         arrived(out.at[at_out, half[c]], fin(c, 0, 0), holder & first)
     for d in (1, 3, 2):
@@ -389,11 +417,7 @@
             z_from = up(z, 4 - e)
             for c in range(2):
                 arrived(out.at[out_rows(z_from, y_from), half[c]], fin(c, e, d), y_from // 2 == s)
-    for c, when in pending:
-        if when is None:
-            c.wait_send()
-        else:
-            pl.when(when)(c.wait_send)
+    flush(len(pending))
 
 
 def on_device(*arrays):
@@ -402,7 +426,7 @@
     return pl.pallas_call(
         kernel,
         out_shape=pltpu.VMEM((512, 1024), BF),
-        in_specs=[hbm, vmem, hbm, hbm, hbm, hbm, pl.BlockSpec(memory_space=pltpu.SMEM)],
+        in_specs=[hbm, hbm, hbm, hbm, hbm, hbm, pl.BlockSpec(memory_space=pltpu.SMEM)],
         out_specs=vmem,
         scratch_shapes=[
             pltpu.VMEM((1024, 512), BF),
@@ -417,12 +441,13 @@
             pltpu.VMEM((2, 8, 128), F32),
             pltpu.VMEM((3, 8, 128), F32),
             pltpu.VMEM((1024, 256), BF),
-            pltpu.VMEM((128, 256), BF),
-            pltpu.VMEM((4, 128, 256), BF),
+            pltpu.VMEM((2, 128, 128), BF),
+            pltpu.VMEM((4, 2, 128, 128), BF),
             pltpu.VMEM((2, 4, 64, 512), BF),
             pltpu.VMEM((2, 3, 64, 512), BF),
             pltpu.VMEM((64, 1024), BF),
             pltpu.VMEM((64, 1024), BF),
+            pltpu.VMEM((1, 4096), F32),
             pltpu.SemaphoreType.DMA((N_SEND,)),
             pltpu.SemaphoreType.DMA((N_RECV,)),
             pltpu.SemaphoreType.DMA((N_LOCAL,)),

time: 82.5 us -> 80.5 us (0.976)
  Pallas kernels: 81.3 us -> 79.4 us
    pallas_call x1, Pallas kernels: 81.3 us -> 79.4 us  [on_device(): pl.pallas_call(kernel, out_shape=pltpu.VMEM((512, 1024), BF), in_specs=[h...]
where the time goes in v3:
time: 80.5 us; the launch traced here: 80.4 us
  Pallas kernels  79.4 us (99%)
  local copies, waits for them, and re-layouts  0.97 us (1%)
    pallas_call x1, Pallas kernels, on_device(): pl.pallas_call(kernel, out_shape=pltpu.VMEM((512, 1024), BF), in_specs=[h...  79.4 us

profile of v3, /device:TPU:1, one launch (start us, length us, event | category | flops | bytes accessed | tf_op | source)
XLA Modules:
  0.0 80.4 jit_solution(7327909917491310525)
XLA Ops:
  0.0 79.4 %shard_map.73 = bf16[512,1024]{1,0:T(8,128)(2,1)S(1)} custom-call(bf16[1024,1024]{1,0:T(8,128)(2,1)} %emb.1, f32[1,4096]{1,0:T(1,128)} %gain.1, bf16[1,256,512]{2,1,0:T(8,128)(2,1)} %wq.1, bf16[1,256,256]{2,1,0:T(8,128)(2,1)} %wk.1, bf16[1,256,256]{2,1,0:T(8,128)(2,1)} %wv.1, bf16[1,128,1024]{2,1,0:T(8,128)(2,1)} %wo.1, s32[8]{0:T(128)} %blocks.1), custom_call_target="tpu_custom_call" | custom-call | tf_op jit(solution)/shard_map/pallas_call | solution.py:426
  79.4 1.0 %copy.9 = bf16[512,1024]{1,0:T(8,128)(2,1)} copy(bf16[512,1024]{1,0:T(8,128)(2,1)S(1)} %shard_map.73) | data formatting | bytes 2097152

commit v4 on v3

--- a/solution.py
+++ b/solution.py
@@ -13,7 +13,7 @@
 D = 4096
 GROUPS = 8
 UNIT = 16
-SCALE = 1.0 / math.sqrt(128)
+SCALE = math.log2(math.e) / math.sqrt(128)
 
 KV_LEFT, KV_RIGHT, KV_FAR = 0, 2, 4
 Q_LEFT, Q_RIGHT, Q_FAR = 6, 8, 10
@@ -24,15 +24,15 @@
 AT_IN = 40
 RO_IN = 48
 RES_IN = 54
-FIN_IN = 56
-N_RECV = 88
-N_SEND = 136
+FZ_IN, FY_IN, REST_IN = 55, 58, 61
+N_RECV = 62
+N_SEND = 104
 N_LOCAL = 8
 
 
 def kernel(
     emb, gain, wq, wk, wv, wo, blocks, out,
-    WKV, WQ, WO, X, XG, PK, PKR, PQ, PQR, SQ, SQR, KV, AT, ATR, OS, OR, RES, ST, GAIN,
+    WKV, WQ, WO, X, XG, ACC, PK, PKR, PQ, PQR, SQ, SQR, KV, AT, ATR, OS, OR, RES, ST, GAIN,
     send_sems, recv_sems, local_sems, go,
 ):
     s = lax.axis_index("section")
@@ -55,16 +55,18 @@
 
     pending = []
 
-    def send(src, dst, ridx, device, when=None):
+    def send(src, dst, ridx, device, when=None, group=None):
         c = pltpu.make_async_remote_copy(
-            src_ref=src, dst_ref=dst, send_sem=send_sems.at[len(pending)],
+            src_ref=src, dst_ref=dst,
+            send_sem=send_sems.at[len(pending) if group is None else N_SEND - 1 - group],
             recv_sem=recv_sems.at[ridx], device_id=device, device_id_type=MESH,
         )
         if when is None:
             c.start()
         else:
             pl.when(when)(c.start)
-        pending.append((c, when))
+        if group is None:
+            pending.append((c, when))
 
     finished = [0]
 
@@ -86,30 +88,22 @@
         else:
             pl.when(when)(c.wait_recv)
 
+    def sent(ref, group, when):
+        c = pltpu.make_async_remote_copy(
+            src_ref=ref, dst_ref=ref, send_sem=send_sems.at[N_SEND - 1 - group],
+            recv_sem=recv_sems.at[0], device_id=dev(1 - s, t, z, y), device_id_type=MESH,
+        )
+        pl.when(when)(c.wait_send)
+
     def rows(start, size):
         return pl.ds(pl.multiple_of(start, size), size)
 
-    KV[...] = jnp.zeros_like(KV)
+    KV[:, 128:256] = jnp.zeros((1024, 128), BF)
 
     barrier = pltpu.get_barrier_semaphore()
 
     def greet(device):
         pl.semaphore_signal(barrier, inc=1, device_id=device, device_id_type=MESH)
-
-    for d in (1, 2, 3):
-        greet(dev(s, t, z, up(y, d)))
-        greet(dev(s, t, up(z, d), y))
-        greet(dev(s, t, z + 1 - 2 * zh, up(y, d)))
-        greet(dev(1 - s, t, z, up(y, d)))
-        greet(dev(1 - s, t, up(z, d), y))
-        greet(dev(s, up(t, d), t, y))
-        greet(dev(s, z, up(z, d), y))
-    greet(dev(1 - s, t, z, y))
-
-    @pl.when(apart)
-    def _():
-        greet(dev(s, t, t, y))
-        greet(dev(s, z, z, y))
 
     for d in range(4):
         @pl.when(first)
@@ -119,6 +113,22 @@
         @pl.when(second)
         def _():
             greet(dev(0, z, d, y))
+    for d in (2, 1, 3):
+        greet(dev(s, up(t, d), t, y))
+        greet(dev(s, z, up(z, d), y))
+
+    @pl.when(apart)
+    def _():
+        greet(dev(s, t, t, y))
+        greet(dev(s, z, z, y))
+    for d in (2, 1, 3):
+        greet(dev(s, t, z + 1 - 2 * zh, up(y, d)))
+        greet(dev(s, t, z, up(y, d)))
+        greet(dev(s, t, up(z, d), y))
+        greet(dev(1 - s, t, z, up(y, d)))
+        greet(dev(1 - s, t, up(z, d), y))
+    greet(dev(1 - s, t, z, y))
+
     at_y = rows(256 * y, 256)
     kc, vc = pl.ds(0, 256), pl.ds(256, 256)
     own = [
@@ -143,17 +153,18 @@
     dev_r, dev_l = dev(s, t, z, right), dev(s, t, z, left)
     at_l, at_r, at_f = rows(256 * left, 256), rows(256 * right, 256), rows(256 * far, 256)
 
+    @pl.when(second)
+    def _():
+        pl.semaphore_wait(go, 1)
+
+    send(wk.at[0], WKV.at[at_y, kc], KV_LEFT, dev_r)
+    send(wv.at[0], WKV.at[at_y, vc], KV_RIGHT + 1, dev_l)
+
     half = (pl.ds(0, 512), pl.ds(512, 512))
     for d in (2, 1, 3):
         send(my_emb, X.at[my_rows], X_IN + z, dev(0, up(t, d), t, y), first)
     send(my_emb, X.at[my_rows], X_IN + z, dev(0, t, t, y), first & apart)
 
-    @pl.when(second)
-    def _():
-        pl.semaphore_wait(go, 1)
-
-    send(wk.at[0], WKV.at[at_y, kc], KV_LEFT, dev_r)
-    send(wv.at[0], WKV.at[at_y, vc], KV_RIGHT + 1, dev_l)
     send(wv.at[0], WKV.at[at_y, vc], KV_LEFT + 1, dev_r)
     send(wk.at[0], WKV.at[at_y, kc], KV_RIGHT, dev_l)
     arrived(WKV.at[at_l, kc], KV_LEFT)
@@ -195,34 +206,46 @@
 
     forward_q(second)
     send_out_weights(second)
-    forward_out_weights(second)
-
-    pl.when(first & diagonal)(own_x.wait)
-    for zp in range(4):
-        place = pl.ds(64 * zp, 64)
-        arrived(X.at[place], X_IN + zp, first & jnp.logical_not(diagonal & (z == zp)))
-    for c in range(2):
-        for zp in range(4):
-            arrived(X.at[pl.ds(64 * zp, 64), half[c]], X_IN + 4 * c + zp, second)
-    for c in own:
-        c.wait()
-    x = X[...].astype(F32)
-    XG[...] = (x * GAIN[:, rows(1024 * z, 1024)]).astype(BF)
+
     def multiply(block, ref):
         at = rows(256 * block, 256)
         return jnp.dot(XG[:, at], ref[at, :], preferred_element_type=F32)
 
-    part = multiply(y, WKV)
-    arrived(WKV.at[at_l, vc], KV_LEFT + 1)
-    part = part + multiply(left, WKV)
-    arrived(WKV.at[at_r, kc], KV_RIGHT)
-    part = part + multiply(right, WKV)
-    arrived(WKV.at[at_f, kc], KV_FAR)
-    arrived(WKV.at[at_f, vc], KV_FAR + 1)
-    part = part + multiply(far, WKV)
+    for c in own:
+        c.wait()
+
+    @pl.when(first)
+    def _():
+        pl.when(diagonal)(own_x.wait)
+        for zp in range(4):
+            arrived(X.at[pl.ds(64 * zp, 64)], X_IN + zp, jnp.logical_not(diagonal & (z == zp)))
+        XG[...] = (X[...].astype(F32) * GAIN[:, rows(1024 * z, 1024)]).astype(BF)
+        part = multiply(y, WKV)
+        arrived(WKV.at[at_l, vc], KV_LEFT + 1)
+        part = part + multiply(left, WKV)
+        arrived(WKV.at[at_r, kc], KV_RIGHT)
+        part = part + multiply(right, WKV)
+        arrived(WKV.at[at_f, kc], KV_FAR)
+        arrived(WKV.at[at_f, vc], KV_FAR + 1)
+        ACC[...] = part + multiply(far, WKV)
+
+    @pl.when(second)
+    def _():
+        arrived(WKV.at[at_l, vc], KV_LEFT + 1)
+        arrived(WKV.at[at_r, kc], KV_RIGHT)
+        arrived(WKV.at[at_f, kc], KV_FAR)
+        arrived(WKV.at[at_f, vc], KV_FAR + 1)
+        for c in range(2):
+            for zp in range(4):
+                arrived(X.at[pl.ds(64 * zp, 64), half[c]], X_IN + 4 * c + zp)
+            scale = GAIN[:, rows(1024 * z + 512 * c, 512)]
+            XG[:, half[c]] = (X[:, half[c]].astype(F32) * scale).astype(BF)
+            part = jnp.dot(XG[:, half[c]], WKV[512 * c:512 * c + 512, :], preferred_element_type=F32)
+            ACC[...] = part + ACC[...] if c else part
+
     for gg in range(2):
         for hh in range(2):
-            rows_of = part[128 * hh:128 * hh + 128]
+            rows_of = ACC[128 * hh:128 * hh + 128, :]
             PK[2 * gg + hh, :, 0:128] = rows_of[:, 128 * gg:128 * gg + 128].astype(BF)
             PK[2 * gg + hh, :, 128:256] = rows_of[:, 256 + 128 * gg:384 + 128 * gg].astype(BF)
     for d in (2, 1, 3):
@@ -231,6 +254,8 @@
 
     forward_q(first)
     send_out_weights(first)
+    forward_out_weights(second)
+    x = X[...].astype(F32)
     squares = jnp.sum(x * x, axis=1, keepdims=True)
     for h in range(2):
         column = jnp.broadcast_to(squares[128 * h:128 * h + 128], (128, 128))
@@ -294,7 +319,7 @@
     for d in (1, 3, 2):
         arrived(PQR.at[d - 1], RQ_IN + d - 1)
         total = total + PQR[d - 1].astype(F32)
-    queries = (total * wide).astype(BF)
+    queries = (total * (wide * SCALE)).astype(BF)
 
     for dy in (1, 3, 2, 0):
         for dz in range(2):
@@ -305,24 +330,26 @@
             theirs = 2 * y_from + h_from
             arrived(KV.at[rows(128 * theirs, 128)], KV_IN + 2 * dy + dz - 1, theirs < block)
 
+    lanes = (pl.ds(0, 128), pl.ds(128, 128))
     keys = KV[:, 0:128]
     values = KV[:, 128:256]
     for h in range(2):
         scores = lax.dot_general(
             queries[:, 128 * h:128 * h + 128], keys, (((1,), (1,)), ((), ())), preferred_element_type=F32
-        ) * SCALE
+        )
         scores = jnp.where(allowed, scores, -jnp.inf)
-        exps = jnp.exp(scores - jnp.max(scores, axis=1, keepdims=True))
+        exps = jnp.exp2(scores - jnp.max(scores, axis=1, keepdims=True))
         norm = jnp.sum(exps, axis=1, keepdims=True)
         heads = jnp.dot(exps.astype(BF), values, preferred_element_type=F32) / norm
         AT[h] = heads.astype(BF)
         for d in (2, 1, 3):
-            send(AT.at[h], ATR.at[z, h], AT_IN + 4 * h + z, dev(s, up(t, d), t, y))
-        send(AT.at[h], ATR.at[z, h], AT_IN + 4 * h + z, dev(s, t, t, y), apart)
+            send(AT.at[h], ATR.at[z, :, lanes[h]], AT_IN + 4 * h + z, dev(s, up(t, d), t, y))
+        send(AT.at[h], ATR.at[z, :, lanes[h]], AT_IN + 4 * h + z, dev(s, t, t, y), apart)
 
     @pl.when(diagonal)
     def _():
-        ATR[z] = AT[...]
+        for h in range(2):
+            ATR[z, :, lanes[h]] = AT[h]
 
     flush(front)
 
@@ -331,20 +358,16 @@
         pl.semaphore_signal(go, inc=1, device_id=dev(1, t, z, y), device_id_type=MESH)
 
     pl.when(first)(own_res.wait)
-    for c in range(2):
-        arrived(RES.at[:, half[c]], RES_IN + c, second)
+    arrived(RES, RES_IN, second)
     arrived(out_part(far, 0), O_FAR)
     arrived(out_part(far, 1), O_FAR + 1)
     for zp in range(4):
         for h in range(2):
-            arrived(ATR.at[zp, h], AT_IN + 4 * h + zp, jnp.logical_not(diagonal & (z == zp)))
+            arrived(ATR.at[zp, :, lanes[h]], AT_IN + 4 * h + zp, jnp.logical_not(diagonal & (z == zp)))
     for c in range(2):
         for hh in range(2):
-            product = jnp.zeros((128, 512), F32)
-            for q in range(4):
-                product = product + jnp.dot(
-                    ATR[2 * (q // 2) + hh, q % 2], WO[128 * q:128 * q + 128, half[c]], preferred_element_type=F32
-                )
+            product = jnp.dot(ATR[hh], WO[0:256, half[c]], preferred_element_type=F32)
+            product = product + jnp.dot(ATR[2 + hh], WO[256:512, half[c]], preferred_element_type=F32)
             OS[c, 2 * hh] = product[0:64].astype(BF)
             OS[c, 2 * hh + 1] = product[64:128].astype(BF)
         for d in (2, 1, 3):
@@ -359,9 +382,6 @@
         return rows(256 * (y_ % 2) + 64 * z_, 64)
 
     at_out = out_rows(z, y)
-
-    def fin(c, dz, dy):
-        return FIN_IN + 16 * c + 4 * dz + dy
 
     for c in range(2):
         new = RES[:, half[c]].astype(F32) + OS[c, z].astype(F32)
@@ -372,21 +392,21 @@
         mine = ST.at[:, half[c]]
         for d in (2, 1, 3, 0):
             send(mine, X.at[my_rows, half[c]], X_IN + 4 * c + z, dev(1, up(t, d), t, y), first)
-        send(mine, RES.at[:, half[c]], RES_IN + c, dev(1, t, z, y), first)
         place = out.at[at_out, half[c]]
         for d in (2, 1, 3):
             if c == 0:
-                send(mine, place, fin(c, d, 0), dev(sec, t, up(z, d), y), second)
+                send(mine, place, FZ_IN + d - 1, dev(sec, t, up(z, d), y), second, 0)
             else:
-                send(mine, place, fin(c, 0, d), dev(sec, t, z, up(y, d)), second)
+                send(mine, place, FY_IN + d - 1, dev(sec, t, z, up(y, d)), second, 0)
     for c in range(2):
         mine, place = ST.at[:, half[c]], out.at[at_out, half[c]]
         for d in (2, 1, 3):
             if c == 0:
-                send(mine, place, fin(c, 0, d), dev(sec, t, z, up(y, d)), second)
+                send(mine, place, REST_IN, dev(sec, t, z, up(y, d)), second, 0)
             else:
-                send(mine, place, fin(c, d, 0), dev(sec, t, up(z, d), y), second)
-        send(mine, place, fin(c, 0, 0), dev(sec, t, z, y), cross)
+                send(mine, place, REST_IN, dev(sec, t, up(z, d), y), second, 0)
+    send(ST, out.at[at_out], REST_IN, dev(sec, t, z, y), cross, 1)
+    send(ST, RES, RES_IN, dev(1, t, z, y), first)
 
     @pl.when(second & (sec == 1))
     def _():
@@ -395,29 +415,24 @@
     holder = sec == s
     for d in (1, 3, 2):
         place = out.at[out_rows(up(z, 4 - d), y), half[0]]
-        arrived(place, fin(0, d, 0), holder)
+        arrived(place, FZ_IN + d - 1, holder)
         for e in (2, 1, 3):
-            send(place, place, fin(0, d, e), dev(s, t, z, up(y, e)), holder)
+            send(place, place, REST_IN, dev(s, t, z, up(y, e)), holder, 2)
         y_from = up(y, 4 - d)
         here = y_from // 2 == s
         place = out.at[out_rows(z, y_from), half[1]]
-        arrived(place, fin(1, 0, d), here)
+        arrived(place, FY_IN + d - 1, here)
         for e in (2, 1, 3):
-            send(place, place, fin(1, e, d), dev(s, t, up(z, e), y), here)
-    flush(summed)
-    for c in range(2):
-        arrived(out.at[at_out, half[c]], fin(c, 0, 0), holder & first)
-    for d in (1, 3, 2):
-        y_from = up(y, 4 - d)
-        arrived(out.at[out_rows(z, y_from), half[0]], fin(0, 0, d), y_from // 2 == s)
-        arrived(out.at[out_rows(up(z, 4 - d), y), half[1]], fin(1, d, 0), holder)
-    for e in (1, 3, 2):
-        for d in (1, 3, 2):
-            y_from = up(y, 4 - d)
-            z_from = up(z, 4 - e)
-            for c in range(2):
-                arrived(out.at[out_rows(z_from, y_from), half[c]], fin(c, e, d), y_from // 2 == s)
+            send(place, place, REST_IN, dev(s, t, up(z, e), y), here, 2)
     flush(len(pending))
+    sent(out.at[0:384], 0, second)
+    sent(out.at[0:64], 1, cross)
+    guest = jnp.logical_not(holder)
+    arrived(out.at[0:320], REST_IN, holder & second)
+    arrived(out.at[0:384], REST_IN, holder & first)
+    arrived(out.at[0:448], REST_IN, guest)
+    sent(out.at[0:384], 2, holder)
+    sent(out.at[0:192], 2, guest)
 
 
 def on_device(*arrays):
@@ -434,6 +449,7 @@
             pltpu.VMEM((512, 1024), BF),
             pltpu.VMEM((256, 1024), BF),
             pltpu.VMEM((256, 1024), BF),
+            pltpu.VMEM((256, 512), F32),
             pltpu.VMEM((4, 128, 256), BF),
             pltpu.VMEM((3, 128, 256), BF),
             pltpu.VMEM((4, 128, 256), BF),
@@ -442,7 +458,7 @@
             pltpu.VMEM((3, 8, 128), F32),
             pltpu.VMEM((1024, 256), BF),
             pltpu.VMEM((2, 128, 128), BF),
-            pltpu.VMEM((4, 2, 128, 128), BF),
+            pltpu.VMEM((4, 128, 256), BF),
             pltpu.VMEM((2, 4, 64, 512), BF),
             pltpu.VMEM((2, 3, 64, 512), BF),
             pltpu.VMEM((64, 1024), BF),

time: 80.5 us -> 78.9 us (0.980)
  Pallas kernels: 79.4 us -> 77.8 us
    pallas_call x1, Pallas kernels: 79.4 us -> 77.8 us  [on_device(): pl.pallas_call(kernel, out_shape=pltpu.VMEM((512, 1024), BF), in_specs=[h...]
where the time goes in v4:
time: 78.9 us; the launch traced here: 78.8 us
  Pallas kernels  77.8 us (99%)
  local copies, waits for them, and re-layouts  0.97 us (1%)
    pallas_call x1, Pallas kernels, on_device(): pl.pallas_call(kernel, out_shape=pltpu.VMEM((512, 1024), BF), in_specs=[h...  77.8 us

profile of v4, /device:TPU:1, one launch (start us, length us, event | category | flops | bytes accessed | tf_op | source)
XLA Modules:
  0.0 78.8 jit_solution(17895979127858074062)
XLA Ops:
  0.0 77.8 %shard_map.73 = bf16[512,1024]{1,0:T(8,128)(2,1)S(1)} custom-call(bf16[1024,1024]{1,0:T(8,128)(2,1)} %emb.1, f32[1,4096]{1,0:T(1,128)} %gain.1, bf16[1,256,512]{2,1,0:T(8,128)(2,1)} %wq.1, bf16[1,256,256]{2,1,0:T(8,128)(2,1)} %wk.1, bf16[1,256,256]{2,1,0:T(8,128)(2,1)} %wv.1, bf16[1,128,1024]{2,1,0:T(8,128)(2,1)} %wo.1, s32[8]{0:T(128)} %blocks.1), custom_call_target="tpu_custom_call" | custom-call | tf_op jit(solution)/shard_map/pallas_call | solution.py:441
  77.8 1.0 %copy.9 = bf16[512,1024]{1,0:T(8,128)(2,1)} copy(bf16[512,1024]{1,0:T(8,128)(2,1)S(1)} %shard_map.73) | data formatting | bytes 2097152

commit v5 on v4

--- a/solution.py
+++ b/solution.py
@@ -18,15 +18,16 @@
 KV_LEFT, KV_RIGHT, KV_FAR = 0, 2, 4
 Q_LEFT, Q_RIGHT, Q_FAR = 6, 8, 10
 O_LEFT, O_RIGHT, O_FAR = 12, 13, 14
-X_IN = 16
+X_IN = 77
 RS_IN, SQ_IN, RQ_IN = 24, 27, 30
-KV_IN = 33
+KV_IN = (33, 70)
 AT_IN = 40
-RO_IN = 48
+RO_IN = 93
 RES_IN = 54
 FZ_IN, FY_IN, REST_IN = 55, 58, 61
-N_RECV = 62
-N_SEND = 104
+FINE = 62
+N_RECV = 105
+N_SEND = 136
 N_LOCAL = 8
 
 
@@ -157,20 +158,28 @@
     def _():
         pl.semaphore_wait(go, 1)
 
-    send(wk.at[0], WKV.at[at_y, kc], KV_LEFT, dev_r)
-    send(wv.at[0], WKV.at[at_y, vc], KV_RIGHT + 1, dev_l)
+    def kv_part(block, h, c):
+        return WKV.at[rows(256 * block + 128 * h, 128), c]
+
+    for h in range(2):
+        send(wk.at[0, pl.ds(128 * h, 128)], kv_part(y, h, kc), FINE + h, dev_r)
+        send(wv.at[0, pl.ds(128 * h, 128)], kv_part(y, h, vc), FINE + 2 + h, dev_l)
 
     half = (pl.ds(0, 512), pl.ds(512, 512))
+    quarter = [pl.ds(256 * c, 256) for c in range(4)]
     for d in (2, 1, 3):
         send(my_emb, X.at[my_rows], X_IN + z, dev(0, up(t, d), t, y), first)
     send(my_emb, X.at[my_rows], X_IN + z, dev(0, t, t, y), first & apart)
 
     send(wv.at[0], WKV.at[at_y, vc], KV_LEFT + 1, dev_r)
     send(wk.at[0], WKV.at[at_y, kc], KV_RIGHT, dev_l)
-    arrived(WKV.at[at_l, kc], KV_LEFT)
-    send(WKV.at[at_l, kc], WKV.at[at_l, kc], KV_FAR, dev_r)
-    arrived(WKV.at[at_r, vc], KV_RIGHT + 1)
-    send(WKV.at[at_r, vc], WKV.at[at_r, vc], KV_FAR + 1, dev_l)
+    for h in range(2):
+        part = kv_part(left, h, kc)
+        arrived(part, FINE + h)
+        send(part, part, FINE + 4 + h, dev_r)
+        part = kv_part(right, h, vc)
+        arrived(part, FINE + 2 + h)
+        send(part, part, FINE + 6 + h, dev_l)
 
     def q_rows(block, h):
         return rows(256 * block + 128 * h, 128)
@@ -225,22 +234,24 @@
         part = part + multiply(left, WKV)
         arrived(WKV.at[at_r, kc], KV_RIGHT)
         part = part + multiply(right, WKV)
-        arrived(WKV.at[at_f, kc], KV_FAR)
-        arrived(WKV.at[at_f, vc], KV_FAR + 1)
+        for h in range(2):
+            arrived(kv_part(far, h, kc), FINE + 4 + h)
+            arrived(kv_part(far, h, vc), FINE + 6 + h)
         ACC[...] = part + multiply(far, WKV)
 
     @pl.when(second)
     def _():
         arrived(WKV.at[at_l, vc], KV_LEFT + 1)
         arrived(WKV.at[at_r, kc], KV_RIGHT)
-        arrived(WKV.at[at_f, kc], KV_FAR)
-        arrived(WKV.at[at_f, vc], KV_FAR + 1)
-        for c in range(2):
+        for h in range(2):
+            arrived(kv_part(far, h, kc), FINE + 4 + h)
+            arrived(kv_part(far, h, vc), FINE + 6 + h)
+        for c in range(4):
             for zp in range(4):
-                arrived(X.at[pl.ds(64 * zp, 64), half[c]], X_IN + 4 * c + zp)
-            scale = GAIN[:, rows(1024 * z + 512 * c, 512)]
-            XG[:, half[c]] = (X[:, half[c]].astype(F32) * scale).astype(BF)
-            part = jnp.dot(XG[:, half[c]], WKV[512 * c:512 * c + 512, :], preferred_element_type=F32)
+                arrived(X.at[pl.ds(64 * zp, 64), quarter[c]], X_IN + 4 * c + zp)
+            scale = GAIN[:, rows(1024 * z + 256 * c, 256)]
+            XG[:, quarter[c]] = (X[:, quarter[c]].astype(F32) * scale).astype(BF)
+            part = jnp.dot(XG[:, quarter[c]], WKV[quarter[c], :], preferred_element_type=F32)
             ACC[...] = part + ACC[...] if c else part
 
     for gg in range(2):
@@ -292,14 +303,23 @@
         total = total + PKR[d - 1].astype(F32)
     block = 2 * y + zh
     KV[rows(128 * block, 128), :] = (total * wide).astype(BF)
-    mine = KV.at[rows(128 * block, 128)]
-    for dy in (2, 1, 3, 0):
-        for dz in range(2):
-            if dy + dz == 0:
-                continue
-            y_to = up(y, dy)
-            h_to = zh if dz == 0 else 1 - zh
-            send(mine, mine, KV_IN + 2 * dy + dz - 1, dev(s, t, 2 * g + h_to, y_to), 2 * y_to + h_to > block)
+    lanes = (pl.ds(0, 128), pl.ds(128, 128))
+
+    def cached(theirs, part):
+        return KV.at[rows(128 * theirs, 128), lanes[part]]
+
+    for part in range(2):
+        for dy in (2, 1, 3, 0):
+            for dz in range(2):
+                if dy + dz == 0:
+                    continue
+                y_to = up(y, dy)
+                h_to = zh if dz == 0 else 1 - zh
+                mine = cached(block, part)
+                send(
+                    mine, mine, KV_IN[part] + 2 * dy + dz - 1,
+                    dev(s, t, 2 * g + h_to, y_to), 2 * y_to + h_to > block,
+                )
     front = len(pending)
 
     places = 256 * y + 128 * zh + lax.broadcasted_iota(jnp.int32, (128, 1), 0)
@@ -321,18 +341,19 @@
         total = total + PQR[d - 1].astype(F32)
     queries = (total * (wide * SCALE)).astype(BF)
 
-    for dy in (1, 3, 2, 0):
-        for dz in range(2):
-            if dy + dz == 0:
-                continue
-            y_from = up(y, 4 - dy)
-            h_from = zh if dz == 0 else 1 - zh
-            theirs = 2 * y_from + h_from
-            arrived(KV.at[rows(128 * theirs, 128)], KV_IN + 2 * dy + dz - 1, theirs < block)
-
-    lanes = (pl.ds(0, 128), pl.ds(128, 128))
+    def wait_cached(part):
+        for dy in (1, 3, 2, 0):
+            for dz in range(2):
+                if dy + dz == 0:
+                    continue
+                y_from = up(y, 4 - dy)
+                h_from = zh if dz == 0 else 1 - zh
+                theirs = 2 * y_from + h_from
+                arrived(cached(theirs, part), KV_IN[part] + 2 * dy + dz - 1, theirs < block)
+
+    wait_cached(0)
     keys = KV[:, 0:128]
-    values = KV[:, 128:256]
+    weights = []
     for h in range(2):
         scores = lax.dot_general(
             queries[:, 128 * h:128 * h + 128], keys, (((1,), (1,)), ((), ())), preferred_element_type=F32
@@ -340,7 +361,12 @@
         scores = jnp.where(allowed, scores, -jnp.inf)
         exps = jnp.exp2(scores - jnp.max(scores, axis=1, keepdims=True))
         norm = jnp.sum(exps, axis=1, keepdims=True)
-        heads = jnp.dot(exps.astype(BF), values, preferred_element_type=F32) / norm
+        weights.append((exps.astype(BF), norm))
+    wait_cached(1)
+    values = KV[:, 128:256]
+    for h in range(2):
+        exps, norm = weights[h]
+        heads = jnp.dot(exps, values, preferred_element_type=F32) / norm
         AT[h] = heads.astype(BF)
         for d in (2, 1, 3):
             send(AT.at[h], ATR.at[z, :, lanes[h]], AT_IN + 4 * h + z, dev(s, up(t, d), t, y))
@@ -364,15 +390,14 @@
     for zp in range(4):
         for h in range(2):
             arrived(ATR.at[zp, :, lanes[h]], AT_IN + 4 * h + zp, jnp.logical_not(diagonal & (z == zp)))
-    for c in range(2):
+    for c in range(4):
         for hh in range(2):
-            product = jnp.dot(ATR[hh], WO[0:256, half[c]], preferred_element_type=F32)
-            product = product + jnp.dot(ATR[2 + hh], WO[256:512, half[c]], preferred_element_type=F32)
+            product = jnp.dot(ATR[hh], WO[0:256, quarter[c]], preferred_element_type=F32)
+            product = product + jnp.dot(ATR[2 + hh], WO[256:512, quarter[c]], preferred_element_type=F32)
             OS[c, 2 * hh] = product[0:64].astype(BF)
             OS[c, 2 * hh + 1] = product[64:128].astype(BF)
         for d in (2, 1, 3):
             send(OS.at[c, up(z, d)], OR.at[c, d - 1], RO_IN + 3 * c + d - 1, dev(s, t, up(z, d), y))
-
     summed = len(pending)
 
     sec = y // 2
@@ -383,18 +408,20 @@
 
     at_out = out_rows(z, y)
 
-    for c in range(2):
-        new = RES[:, half[c]].astype(F32) + OS[c, z].astype(F32)
+    for c in range(4):
+        new = RES[:, quarter[c]].astype(F32) + OS[c, z].astype(F32)
         for d in (1, 3, 2):
             arrived(OR.at[c, d - 1], RO_IN + 3 * c + d - 1)
             new = new + OR[c, d - 1].astype(F32)
-        ST[:, half[c]] = new.astype(BF)
-        mine = ST.at[:, half[c]]
+        ST[:, quarter[c]] = new.astype(BF)
+        mine = ST.at[:, quarter[c]]
         for d in (2, 1, 3, 0):
-            send(mine, X.at[my_rows, half[c]], X_IN + 4 * c + z, dev(1, up(t, d), t, y), first)
-        place = out.at[at_out, half[c]]
+            send(mine, X.at[my_rows, quarter[c]], X_IN + 4 * c + z, dev(1, up(t, d), t, y), first)
+        if c % 2 == 0:
+            continue
+        mine, place = ST.at[:, half[c // 2]], out.at[at_out, half[c // 2]]
         for d in (2, 1, 3):
-            if c == 0:
+            if c == 1:
                 send(mine, place, FZ_IN + d - 1, dev(sec, t, up(z, d), y), second, 0)
             else:
                 send(mine, place, FY_IN + d - 1, dev(sec, t, z, up(y, d)), second, 0)
@@ -424,6 +451,7 @@
         arrived(place, FY_IN + d - 1, here)
         for e in (2, 1, 3):
             send(place, place, REST_IN, dev(s, t, up(z, e), y), here, 2)
+    assert len(pending) <= N_SEND - 3
     flush(len(pending))
     sent(out.at[0:384], 0, second)
     sent(out.at[0:64], 1, cross)
@@ -459,8 +487,8 @@
             pltpu.VMEM((1024, 256), BF),
             pltpu.VMEM((2, 128, 128), BF),
             pltpu.VMEM((4, 128, 256), BF),
-            pltpu.VMEM((2, 4, 64, 512), BF),
-            pltpu.VMEM((2, 3, 64, 512), BF),
+            pltpu.VMEM((4, 4, 64, 256), BF),
+            pltpu.VMEM((4, 3, 64, 256), BF),
             pltpu.VMEM((64, 1024), BF),
             pltpu.VMEM((64, 1024), BF),
             pltpu.VMEM((1, 4096), F32),

time: 78.9 us -> 77.4 us (0.981)
  Pallas kernels: 77.8 us -> 76.3 us
    pallas_call x1, Pallas kernels: 77.8 us -> 76.3 us  [on_device(): pl.pallas_call(kernel, out_shape=pltpu.VMEM((512, 1024), BF), in_specs=[h...]
where the time goes in v5:
time: 77.4 us; the launch traced here: 77.2 us
  Pallas kernels  76.3 us (99%)
  local copies, waits for them, and re-layouts  0.97 us (1%)
    pallas_call x1, Pallas kernels, on_device(): pl.pallas_call(kernel, out_shape=pltpu.VMEM((512, 1024), BF), in_specs=[h...  76.3 us

profile of v5, /device:TPU:1, one launch (start us, length us, event | category | flops | bytes accessed | tf_op | source)
XLA Modules:
  0.0 77.2 jit_solution(10587837133942274155)
XLA Ops:
  0.0 76.3 %shard_map.73 = bf16[512,1024]{1,0:T(8,128)(2,1)S(1)} custom-call(bf16[1024,1024]{1,0:T(8,128)(2,1)} %emb.1, f32[1,4096]{1,0:T(1,128)} %gain.1, bf16[1,256,512]{2,1,0:T(8,128)(2,1)} %wq.1, bf16[1,256,256]{2,1,0:T(8,128)(2,1)} %wk.1, bf16[1,256,256]{2,1,0:T(8,128)(2,1)} %wv.1, bf16[1,128,1024]{2,1,0:T(8,128)(2,1)} %wo.1, s32[8]{0:T(128)} %blocks.1), custom_call_target="tpu_custom_call" | custom-call | tf_op jit(solution)/shard_map/pallas_call | solution.py:469
  76.3 1.0 %copy.9 = bf16[512,1024]{1,0:T(8,128)(2,1)} copy(bf16[512,1024]{1,0:T(8,128)(2,1)S(1)} %shard_map.73) | data formatting | bytes 2097152

commit v6 on v5

--- a/solution.py
+++ b/solution.py
@@ -13,21 +13,22 @@
 D = 4096
 GROUPS = 8
 UNIT = 16
+LARGEST = 3.0e38
 SCALE = math.log2(math.e) / math.sqrt(128)
 
 KV_LEFT, KV_RIGHT, KV_FAR = 0, 2, 4
 Q_LEFT, Q_RIGHT, Q_FAR = 6, 8, 10
 O_LEFT, O_RIGHT, O_FAR = 12, 13, 14
 X_IN = 77
-RS_IN, SQ_IN, RQ_IN = 24, 27, 30
+RS_IN, SQ_IN, RQ_IN = (24, 105), 27, 30
 KV_IN = (33, 70)
 AT_IN = 40
 RO_IN = 93
 RES_IN = 54
 FZ_IN, FY_IN, REST_IN = 55, 58, 61
 FINE = 62
-N_RECV = 105
-N_SEND = 136
+N_RECV = 108
+N_SEND = 140
 N_LOCAL = 8
 
 
@@ -216,9 +217,25 @@
     forward_q(second)
     send_out_weights(second)
 
-    def multiply(block, ref):
+    def multiply(block, ref, columns):
         at = rows(256 * block, 256)
-        return jnp.dot(XG[:, at], ref[at, :], preferred_element_type=F32)
+        return jnp.dot(XG[:, at], ref[at, columns], preferred_element_type=F32)
+
+    def pack(part):
+        for gg in range(2):
+            for hh in range(2):
+                piece = ACC[128 * hh:128 * hh + 128, 256 * part + 128 * gg:256 * part + 128 * gg + 128]
+                PK[part, 2 * gg + hh] = piece.astype(BF)
+        for d in (2, 1, 3):
+            other = up(z, d)
+            send(PK.at[part, other], PKR.at[part, d - 1], RS_IN[part] + d - 1, dev(s, t, other, y))
+
+    def scale_rows(squares):
+        scale = lax.rsqrt(squares * (1.0 / D) + 1e-5)
+        XG[...] = (X[...].astype(F32) * scale * GAIN[:, rows(1024 * z, 1024)]).astype(BF)
+        for h in range(2):
+            column = jnp.broadcast_to(squares[128 * h:128 * h + 128], (128, 128))
+            SQ[h] = jnp.transpose(column)[0:8]
 
     for c in own:
         c.wait()
@@ -228,16 +245,14 @@
         pl.when(diagonal)(own_x.wait)
         for zp in range(4):
             arrived(X.at[pl.ds(64 * zp, 64)], X_IN + zp, jnp.logical_not(diagonal & (z == zp)))
-        XG[...] = (X[...].astype(F32) * GAIN[:, rows(1024 * z, 1024)]).astype(BF)
-        part = multiply(y, WKV)
-        arrived(WKV.at[at_l, vc], KV_LEFT + 1)
-        part = part + multiply(left, WKV)
+        x = X[...].astype(F32)
+        scale_rows(jnp.sum(x * x, axis=1, keepdims=True))
+        part = multiply(y, WKV, kc) + multiply(left, WKV, kc)
         arrived(WKV.at[at_r, kc], KV_RIGHT)
-        part = part + multiply(right, WKV)
+        part = part + multiply(right, WKV, kc)
         for h in range(2):
             arrived(kv_part(far, h, kc), FINE + 4 + h)
-            arrived(kv_part(far, h, vc), FINE + 6 + h)
-        ACC[...] = part + multiply(far, WKV)
+        ACC[:, kc] = part + multiply(far, WKV, kc)
 
     @pl.when(second)
     def _():
@@ -246,43 +261,45 @@
         for h in range(2):
             arrived(kv_part(far, h, kc), FINE + 4 + h)
             arrived(kv_part(far, h, vc), FINE + 6 + h)
+        squares = jnp.zeros((256, 1), F32)
         for c in range(4):
             for zp in range(4):
                 arrived(X.at[pl.ds(64 * zp, 64), quarter[c]], X_IN + 4 * c + zp)
-            scale = GAIN[:, rows(1024 * z + 256 * c, 256)]
-            XG[:, quarter[c]] = (X[:, quarter[c]].astype(F32) * scale).astype(BF)
-            part = jnp.dot(XG[:, quarter[c]], WKV[quarter[c], :], preferred_element_type=F32)
-            ACC[...] = part + ACC[...] if c else part
-
-    for gg in range(2):
-        for hh in range(2):
-            rows_of = ACC[128 * hh:128 * hh + 128, :]
-            PK[2 * gg + hh, :, 0:128] = rows_of[:, 128 * gg:128 * gg + 128].astype(BF)
-            PK[2 * gg + hh, :, 128:256] = rows_of[:, 256 + 128 * gg:384 + 128 * gg].astype(BF)
-    for d in (2, 1, 3):
-        other = up(z, d)
-        send(PK.at[other], PKR.at[d - 1], RS_IN + d - 1, dev(s, t, other, y))
-
-    forward_q(first)
-    send_out_weights(first)
-    forward_out_weights(second)
-    x = X[...].astype(F32)
-    squares = jnp.sum(x * x, axis=1, keepdims=True)
-    for h in range(2):
-        column = jnp.broadcast_to(squares[128 * h:128 * h + 128], (128, 128))
-        SQ[h] = jnp.transpose(column)[0:8]
+            x = X[:, quarter[c]].astype(F32)
+            squares = squares + jnp.sum(x * x, axis=1, keepdims=True)
+        scale_rows(squares)
+        ACC[:, kc] = jnp.dot(XG[...], WKV[:, kc], preferred_element_type=F32)
+
     for d in (2, 1, 3):
         other = up(z, d)
         send(SQ.at[other % 2], SQR.at[d - 1], SQ_IN + d - 1, dev(s, t, other, y))
-
-    part = multiply(y, WQ)
+    pack(0)
+
+    @pl.when(first)
+    def _():
+        arrived(WKV.at[at_l, vc], KV_LEFT + 1)
+        part = multiply(y, WKV, vc) + multiply(left, WKV, vc) + multiply(right, WKV, vc)
+        for h in range(2):
+            arrived(kv_part(far, h, vc), FINE + 6 + h)
+        ACC[:, vc] = part + multiply(far, WKV, vc)
+
+    @pl.when(second)
+    def _():
+        ACC[:, vc] = jnp.dot(XG[...], WKV[:, vc], preferred_element_type=F32)
+
+    pack(1)
+
+    forward_q(first)
+    send_out_weights(first)
+    all_q = pl.ds(0, 512)
+    part = multiply(y, WQ, all_q)
     arrived(WQ.at[q_rows(left, 1)], Q_LEFT + 1)
-    part = part + multiply(left, WQ)
+    part = part + multiply(left, WQ, all_q)
     arrived(WQ.at[q_rows(right, 0)], Q_RIGHT)
-    part = part + multiply(right, WQ)
+    part = part + multiply(right, WQ, all_q)
     arrived(WQ.at[q_rows(far, 0)], Q_FAR)
     arrived(WQ.at[q_rows(far, 1)], Q_FAR + 1)
-    part = part + multiply(far, WQ)
+    part = part + multiply(far, WQ, all_q)
     for gg in range(2):
         for hh in range(2):
             PQ[2 * gg + hh] = part[128 * hh:128 * hh + 128, 256 * gg:256 * gg + 256].astype(BF)
@@ -290,32 +307,34 @@
         other = up(z, d)
         send(PQ.at[other], PQR.at[d - 1], RQ_IN + d - 1, dev(s, t, other, y))
 
-    square = SQ[zh]
-    for d in (1, 3, 2):
+    means = [SQ[zh] * (1.0 / D)]
+    for d in (1, 2, 3):
         arrived(SQR.at[d - 1], SQ_IN + d - 1)
-        square = square + SQR[d - 1]
-    inverse_row = lax.rsqrt(square * (1.0 / D) + 1e-5)
-    inverse = jnp.transpose(jnp.broadcast_to(inverse_row[0:1], (128, 128)))
-    wide = jnp.concatenate([inverse, inverse], axis=1)
-    total = PK[z].astype(F32)
-    for d in (1, 3, 2):
-        arrived(PKR.at[d - 1], RS_IN + d - 1)
-        total = total + PKR[d - 1].astype(F32)
+        means.append(SQR[d - 1] * (1.0 / D))
+    inverse = lax.rsqrt(means[0] + means[1] + means[2] + means[3] + 1e-5)
+    shares = []
+    for mean in means:
+        share = inverse * jnp.sqrt(jnp.minimum(mean + 1e-5, LARGEST))
+        shares.append(jnp.transpose(jnp.broadcast_to(share[0:1], (128, 128))))
     block = 2 * y + zh
-    KV[rows(128 * block, 128), :] = (total * wide).astype(BF)
     lanes = (pl.ds(0, 128), pl.ds(128, 128))
 
     def cached(theirs, part):
         return KV.at[rows(128 * theirs, 128), lanes[part]]
 
     for part in range(2):
+        total = PK[part, z].astype(F32) * shares[0]
+        for d in (1, 3, 2):
+            arrived(PKR.at[part, d - 1], RS_IN[part] + d - 1)
+            total = total + PKR[part, d - 1].astype(F32) * shares[d]
+        mine = cached(block, part)
+        mine[...] = total.astype(BF)
         for dy in (2, 1, 3, 0):
             for dz in range(2):
                 if dy + dz == 0:
                     continue
                 y_to = up(y, dy)
                 h_to = zh if dz == 0 else 1 - zh
-                mine = cached(block, part)
                 send(
                     mine, mine, KV_IN[part] + 2 * dy + dz - 1,
                     dev(s, t, 2 * g + h_to, y_to), 2 * y_to + h_to > block,
@@ -335,11 +354,13 @@
     allowed = (keys_at <= places) & (keys_at >= lowest)
 
     forward_out_weights(first)
-    total = PQ[z].astype(F32)
+    forward_out_weights(second)
+    wide = [jnp.concatenate([share, share], axis=1) for share in shares]
+    total = PQ[z].astype(F32) * wide[0]
     for d in (1, 3, 2):
         arrived(PQR.at[d - 1], RQ_IN + d - 1)
-        total = total + PQR[d - 1].astype(F32)
-    queries = (total * (wide * SCALE)).astype(BF)
+        total = total + PQR[d - 1].astype(F32) * wide[d]
+    queries = (total * SCALE).astype(BF)
 
     def wait_cached(part):
         for dy in (1, 3, 2, 0):
@@ -478,8 +499,8 @@
             pltpu.VMEM((256, 1024), BF),
             pltpu.VMEM((256, 1024), BF),
             pltpu.VMEM((256, 512), F32),
-            pltpu.VMEM((4, 128, 256), BF),
-            pltpu.VMEM((3, 128, 256), BF),
+            pltpu.VMEM((2, 4, 128, 128), BF),
+            pltpu.VMEM((2, 3, 128, 128), BF),
             pltpu.VMEM((4, 128, 256), BF),
             pltpu.VMEM((3, 128, 256), BF),
             pltpu.VMEM((2, 8, 128), F32),

time: 77.4 us -> 77.6 us (level)
  no operation moved by 1% of the time
where the time goes in v6:
time: 77.6 us; the launch traced here: 77.5 us
  Pallas kernels  76.5 us (99%)
  local copies, waits for them, and re-layouts  0.97 us (1%)
    pallas_call x1, Pallas kernels, on_device(): pl.pallas_call(kernel, out_shape=pltpu.VMEM((512, 1024), BF), in_specs=[h...  76.5 us

profile of v6, /device:TPU:1, one launch (start us, length us, event | category | flops | bytes accessed | tf_op | source)
XLA Modules:
  0.0 77.5 jit_solution(8869967768672159636)
XLA Ops:
  0.0 76.5 %shard_map.73 = bf16[512,1024]{1,0:T(8,128)(2,1)S(1)} custom-call(bf16[1024,1024]{1,0:T(8,128)(2,1)} %emb.1, f32[1,4096]{1,0:T(1,128)} %gain.1, bf16[1,256,512]{2,1,0:T(8,128)(2,1)} %wq.1, bf16[1,256,256]{2,1,0:T(8,128)(2,1)} %wk.1, bf16[1,256,256]{2,1,0:T(8,128)(2,1)} %wv.1, bf16[1,128,1024]{2,1,0:T(8,128)(2,1)} %wo.1, s32[8]{0:T(128)} %blocks.1), custom_call_target="tpu_custom_call" | custom-call | tf_op jit(solution)/shard_map/pallas_call | solution.py:490
  76.5 1.0 %copy.9 = bf16[512,1024]{1,0:T(8,128)(2,1)} copy(bf16[512,1024]{1,0:T(8,128)(2,1)S(1)} %shard_map.73) | data formatting | bytes 2097152

commit v7 on v6

--- a/solution.py
+++ b/solution.py
@@ -337,7 +337,7 @@
                 h_to = zh if dz == 0 else 1 - zh
                 send(
                     mine, mine, KV_IN[part] + 2 * dy + dz - 1,
-                    dev(s, t, 2 * g + h_to, y_to), 2 * y_to + h_to > block,
+                    dev(s, t, 2 * g + h_to, y_to), (2 * y_to + h_to > block) & (2 * y_to + h_to < block + 7),
                 )
     front = len(pending)
 
@@ -354,7 +354,6 @@
     allowed = (keys_at <= places) & (keys_at >= lowest)
 
     forward_out_weights(first)
-    forward_out_weights(second)
     wide = [jnp.concatenate([share, share], axis=1) for share in shares]
     total = PQ[z].astype(F32) * wide[0]
     for d in (1, 3, 2):
@@ -370,7 +369,7 @@
                 y_from = up(y, 4 - dy)
                 h_from = zh if dz == 0 else 1 - zh
                 theirs = 2 * y_from + h_from
-                arrived(cached(theirs, part), KV_IN[part] + 2 * dy + dz - 1, theirs < block)
+                arrived(cached(theirs, part), KV_IN[part] + 2 * dy + dz - 1, (theirs < block) & (theirs > block - 7))
 
     wait_cached(0)
     keys = KV[:, 0:128]
@@ -398,6 +397,7 @@
         for h in range(2):
             ATR[z, :, lanes[h]] = AT[h]
 
+    forward_out_weights(second)
     flush(front)
 
     @pl.when(first)

time: 77.6 us -> 77.4 us (level)
  no operation moved by 1% of the time
where the time goes in v7:
time: 77.4 us; the launch traced here: 77.3 us
  Pallas kernels  76.3 us (99%)
  local copies, waits for them, and re-layouts  0.97 us (1%)
    pallas_call x1, Pallas kernels, on_device(): pl.pallas_call(kernel, out_shape=pltpu.VMEM((512, 1024), BF), in_specs=[h...  76.3 us

profile of v7, /device:TPU:1, one launch (start us, length us, event | category | flops | bytes accessed | tf_op | source)
XLA Modules:
  0.0 77.3 jit_solution(7786043806919096311)
XLA Ops:
  0.0 76.3 %shard_map.73 = bf16[512,1024]{1,0:T(8,128)(2,1)S(1)} custom-call(bf16[1024,1024]{1,0:T(8,128)(2,1)} %emb.1, f32[1,4096]{1,0:T(1,128)} %gain.1, bf16[1,256,512]{2,1,0:T(8,128)(2,1)} %wq.1, bf16[1,256,256]{2,1,0:T(8,128)(2,1)} %wk.1, bf16[1,256,256]{2,1,0:T(8,128)(2,1)} %wv.1, bf16[1,128,1024]{2,1,0:T(8,128)(2,1)} %wo.1, s32[8]{0:T(128)} %blocks.1), custom_call_target="tpu_custom_call" | custom-call | tf_op jit(solution)/shard_map/pallas_call | solution.py:490
  76.3 1.0 %copy.9 = bf16[512,1024]{1,0:T(8,128)(2,1)} copy(bf16[512,1024]{1,0:T(8,128)(2,1)S(1)} %shard_map.73) | data formatting | bytes 2097152

commit v8 on v7

--- a/solution.py
+++ b/solution.py
@@ -130,6 +130,11 @@
         greet(dev(1 - s, t, z, up(y, d)))
         greet(dev(1 - s, t, up(z, d), y))
     greet(dev(1 - s, t, z, y))
+    greet(dev(1 - s, t, up(z, 2), up(y, 2)))
+
+    @pl.when(second)
+    def _():
+        greet(dev(1, t, up(z, 2), up(y, 2)))
 
     at_y = rows(256 * y, 256)
     kc, vc = pl.ds(0, 256), pl.ds(256, 256)
@@ -149,7 +154,7 @@
     pl.when(first & diagonal)(own_x.start)
     pl.when(first)(own_res.start)
 
-    pl.semaphore_wait(barrier, 26 + 2 * (1 - diagonal.astype(jnp.int32)))
+    pl.semaphore_wait(barrier, 27 + s + 2 * (1 - diagonal.astype(jnp.int32)))
 
     right, left, far = up(y, 1), up(y, 3), up(y, 2)
     dev_r, dev_l = dev(s, t, z, right), dev(s, t, z, left)
@@ -453,6 +458,7 @@
                 send(mine, place, REST_IN, dev(sec, t, z, up(y, d)), second, 0)
             else:
                 send(mine, place, REST_IN, dev(sec, t, up(z, d), y), second, 0)
+    send(ST, out.at[at_out], REST_IN, dev(sec, t, up(z, 2), up(y, 2)), second)
     send(ST, out.at[at_out], REST_IN, dev(sec, t, z, y), cross, 1)
     send(ST, RES, RES_IN, dev(1, t, z, y), first)
 
@@ -464,13 +470,13 @@
     for d in (1, 3, 2):
         place = out.at[out_rows(up(z, 4 - d), y), half[0]]
         arrived(place, FZ_IN + d - 1, holder)
-        for e in (2, 1, 3):
+        for e in (2, 1, 3) if d != 2 else (1, 3):
             send(place, place, REST_IN, dev(s, t, z, up(y, e)), holder, 2)
         y_from = up(y, 4 - d)
         here = y_from // 2 == s
         place = out.at[out_rows(z, y_from), half[1]]
         arrived(place, FY_IN + d - 1, here)
-        for e in (2, 1, 3):
+        for e in (2, 1, 3) if d != 2 else (1, 3):
             send(place, place, REST_IN, dev(s, t, up(z, e), y), here, 2)
     assert len(pending) <= N_SEND - 3
     flush(len(pending))
@@ -480,8 +486,8 @@
     arrived(out.at[0:320], REST_IN, holder & second)
     arrived(out.at[0:384], REST_IN, holder & first)
     arrived(out.at[0:448], REST_IN, guest)
-    sent(out.at[0:384], 2, holder)
-    sent(out.at[0:192], 2, guest)
+    sent(out.at[0:352], 2, holder)
+    sent(out.at[0:160], 2, guest)
 
 
 def on_device(*arrays):

time: 77.4 us -> 77.9 us (level)
  no operation moved by 1% of the time
where the time goes in v8:
time: 77.9 us; the launch traced here: 77.8 us
  Pallas kernels  76.8 us (99%)
  local copies, waits for them, and re-layouts  0.97 us (1%)
    pallas_call x1, Pallas kernels, on_device(): pl.pallas_call(kernel, out_shape=pltpu.VMEM((512, 1024), BF), in_specs=[h...  76.8 us

profile of v8, /device:TPU:1, one launch (start us, length us, event | category | flops | bytes accessed | tf_op | source)
XLA Modules:
  0.0 77.8 jit_solution(12878692370975733654)
XLA Ops:
  0.0 76.8 %shard_map.73 = bf16[512,1024]{1,0:T(8,128)(2,1)S(1)} custom-call(bf16[1024,1024]{1,0:T(8,128)(2,1)} %emb.1, f32[1,4096]{1,0:T(1,128)} %gain.1, bf16[1,256,512]{2,1,0:T(8,128)(2,1)} %wq.1, bf16[1,256,256]{2,1,0:T(8,128)(2,1)} %wk.1, bf16[1,256,256]{2,1,0:T(8,128)(2,1)} %wv.1, bf16[1,128,1024]{2,1,0:T(8,128)(2,1)} %wo.1, s32[8]{0:T(128)} %blocks.1), custom_call_target="tpu_custom_call" | custom-call | tf_op jit(solution)/shard_map/pallas_call | solution.py:496
  76.8 1.0 %copy.9 = bf16[512,1024]{1,0:T(8,128)(2,1)} copy(bf16[512,1024]{1,0:T(8,128)(2,1)S(1)} %shard_map.73) | data formatting | bytes 2097152

commit v9 on v7

--- a/solution.py
+++ b/solution.py
@@ -354,6 +354,7 @@
     allowed = (keys_at <= places) & (keys_at >= lowest)
 
     forward_out_weights(first)
+    forward_out_weights(second)
     wide = [jnp.concatenate([share, share], axis=1) for share in shares]
     total = PQ[z].astype(F32) * wide[0]
     for d in (1, 3, 2):
@@ -397,7 +398,6 @@
         for h in range(2):
             ATR[z, :, lanes[h]] = AT[h]
 
-    forward_out_weights(second)
     flush(front)
 
     @pl.when(first)

time: 77.4 us -> 77.3 us (level)
  no operation moved by 1% of the time
where the time goes in v9:
time: 77.3 us; the launch traced here: 77.2 us
  Pallas kernels  76.2 us (99%)
  local copies, waits for them, and re-layouts  0.97 us (1%)
    pallas_call x1, Pallas kernels, on_device(): pl.pallas_call(kernel, out_shape=pltpu.VMEM((512, 1024), BF), in_specs=[h...  76.2 us

profile of v9, /device:TPU:1, one launch (start us, length us, event | category | flops | bytes accessed | tf_op | source)
XLA Modules:
  0.0 77.2 jit_solution(12330921479598886965)
XLA Ops:
  0.0 76.2 %shard_map.73 = bf16[512,1024]{1,0:T(8,128)(2,1)S(1)} custom-call(bf16[1024,1024]{1,0:T(8,128)(2,1)} %emb.1, f32[1,4096]{1,0:T(1,128)} %gain.1, bf16[1,256,512]{2,1,0:T(8,128)(2,1)} %wq.1, bf16[1,256,256]{2,1,0:T(8,128)(2,1)} %wk.1, bf16[1,256,256]{2,1,0:T(8,128)(2,1)} %wv.1, bf16[1,128,1024]{2,1,0:T(8,128)(2,1)} %wo.1, s32[8]{0:T(128)} %blocks.1), custom_call_target="tpu_custom_call" | custom-call | tf_op jit(solution)/shard_map/pallas_call | solution.py:490
  76.2 1.0 %copy.9 = bf16[512,1024]{1,0:T(8,128)(2,1)} copy(bf16[512,1024]{1,0:T(8,128)(2,1)S(1)} %shard_map.73) | data formatting | bytes 2097152
